TPU v7x, 32 devices: a whole 2x2x4 slice. The times are simulated.
32 devices in a mesh: seq: 2 (over core), dp: 4 (over y, x), tensor: 4 (over z).
Axes of the slice: x: 2, y: 2, z: 4, core: 2. Of those that a mesh axis runs over, the one named last changes fastest.
Arguments:
- attention_queries: bfloat16 [4, 256, 3584], P('dp', 'seq', 'tensor')
- attention_keys: bfloat16 [4, 256, 512], P('dp', 'seq', 'tensor')
- attention_values: bfloat16 [4, 256, 512], P('dp', 'seq', 'tensor')
- key_window_length: int32 [4], P('tensor'), may hold values from 128 to 512, as said below
- norm_gain: float32 [3584], P('tensor'), may hold values from 0.5 to 2
- spike_levels: int32 [3584], P('tensor'), may hold values from 1 to 4
- lin_queries: bfloat16 [4, 256, 3584], P('dp', 'seq', 'tensor'), may hold values from -6 to 6
- lin_keys: bfloat16 [4, 256, 3584], P('dp', 'seq', 'tensor'), may hold values from -6 to 6
- decay_logs: float32 [4, 28, 256], P('dp', 'tensor', 'seq'), as said below
- cotangent: bfloat16 [4, 256, 3584], P('dp', 'seq', 'tensor')
Outputs:
- layer_output: bfloat16 [4, 256, 3584], P('dp', 'seq', 'tensor')
- query_grads: bfloat16 [4, 256, 3584], P('dp', 'seq', 'tensor')
- key_gradient: bfloat16 [4, 256, 512], P('dp', 'seq', 'tensor')
- value_gradient: bfloat16 [4, 256, 512], P('dp', 'seq', 'tensor')
- gain_grads: float32 [3584], P('tensor')
Inputs may be any that keep to these rules, and one draw needn't show every extreme that they name: Key head g lets query t see positions j with t - key_window_length[g] < j <= t; some head has exactly 512. `decay_logs`: non-positive.
All inputs are finite; a program needn't handle non-finite values.
Results may differ from a plain program's by a relative error of at most 0.015.
Values may be sent and summed in bfloat16 or wider, within the bound.
A program may use at most 128 MiB of HBM per device.

v0:
```python
import math

import jax
import jax.numpy as jnp
from jax import lax
from jax.sharding import PartitionSpec as P

HEAD_SIZE = 128
D = 3584
LONGEST_WINDOW = 512


precise = lax.Precision.HIGHEST
epsilon = 1e-06


def passed_along(block, axis, distance):
    devices = range(lax.axis_size(axis))
    route = [(i - distance, i) for i in devices if i - distance in devices]
    return lax.ppermute(block, axis, route)


def entering(value, axis, join, neutral, backward):
    count, mine = (lax.axis_size(axis), lax.axis_index(axis))
    pieces = jax.tree.map(lambda part: lax.all_gather(part, axis), value)
    if backward:
        pieces = jax.tree.map(lambda part: part[::-1], pieces)
        mine = count - 1 - mine
    running = jax.tree.map(
        lambda part, zero: jnp.full_like(part, 0) + jnp.asarray(zero, part.dtype), value, neutral
    )

    def turn(position, running):
        longer = join(running, jax.tree.map(lambda part: part[position], pieces))
        return jax.tree.map(lambda new, old: jnp.where(position < mine, new, old), longer, running)

    return lax.fori_loop(0, count - 1, turn, running)


def head_logits(query_rows, key_row_block, first_query, key_reach, scaling):
    block_rows = query_rows.shape[0]
    key_span = key_row_block.shape[0] - block_rows
    logits = (
        jnp.einsum("sd,kd->sk", query_rows, key_row_block, preferred_element_type=jnp.float32)
        * scaling
    )
    query_pos = first_query + jnp.arange(block_rows, dtype=jnp.int32)[:, None]
    key_pos = first_query - key_span + jnp.arange(key_row_block.shape[0], dtype=jnp.int32)[None, :]
    allowed = (key_pos >= 0) & (key_pos <= query_pos) & (key_pos > query_pos - key_reach)
    return jnp.where(allowed, logits, -jnp.inf)


def chain_states(earlier, later):
    return (earlier[0] * later[0], later[0][:, None, None] * earlier[1] + later[1])


def local(
    attention_queries,
    attention_keys,
    attention_values,
    key_window_length,
    norm_gain,
    spike_levels,
    lin_queries,
    lin_keys,
    decay_logs,
    cotangent,
):
    block_rows = attention_queries.shape[1]
    q_heads = attention_queries.shape[2] // HEAD_SIZE
    kv_heads = attention_keys.shape[2] // HEAD_SIZE
    head_groups = q_heads // kv_heads
    previous = (LONGEST_WINDOW + block_rows - 1) // block_rows
    key_span = previous * block_rows
    first_query = lax.axis_index("seq") * block_rows
    scaling = 1.0 / math.sqrt(HEAD_SIZE)
    own_pair = jnp.stack([attention_keys, attention_values])
    earlier_blocks = []
    moving = own_pair
    for distance in range(previous):
        moving = passed_along(moving, "seq", 1)
        earlier_blocks.append(moving)
    window_pair = jnp.concatenate(earlier_blocks[::-1] + [own_pair], axis=2)
    window_pair = window_pair.reshape(2, key_span + block_rows, kv_heads, HEAD_SIZE).transpose(
        0, 2, 1, 3
    )
    window_keys = window_pair[0]
    window_values = window_pair[1]
    head_queries = attention_queries[0].reshape(block_rows, q_heads, HEAD_SIZE).transpose(1, 0, 2)
    kv_of_head = jnp.arange(q_heads, dtype=jnp.int32) // head_groups

    def forward_head(operands):
        query_rows, kv_index = operands
        key_row_block = lax.dynamic_index_in_dim(window_keys, kv_index, 0, keepdims=False)
        value_rows = lax.dynamic_index_in_dim(window_values, kv_index, 0, keepdims=False)
        key_reach = lax.dynamic_index_in_dim(key_window_length, kv_index, 0, keepdims=False)
        logits = head_logits(query_rows, key_row_block, first_query, key_reach, scaling)
        row_max = jnp.max(logits, axis=-1)
        exponent = jnp.exp(logits - row_max[:, None])
        row_sum = jnp.sum(exponent, axis=-1)
        weights = (exponent / row_sum[:, None]).astype(jnp.bfloat16)
        head_output = jnp.dot(weights, value_rows, preferred_element_type=jnp.float32).astype(
            jnp.bfloat16
        )
        return (head_output, row_max, row_sum)

    heads_out, maxima, sums = lax.map(forward_head, (head_queries, kv_of_head))
    out_float = heads_out.astype(jnp.float32)
    square_sum = lax.psum(jnp.sum(out_float * out_float, axis=(0, 2)), "tensor")
    inverse = 1.0 / jnp.sqrt(square_sum / D + epsilon)
    normed = out_float * inverse[None, :, None]
    gain_rows = norm_gain.reshape(q_heads, HEAD_SIZE)[:, None, :]
    ceiling = spike_levels.astype(jnp.float32).reshape(q_heads, HEAD_SIZE)[:, None, :]
    bounded = jnp.tanh(normed * gain_rows / ceiling)
    spikes = (ceiling * bounded).astype(jnp.bfloat16)
    membrane_queries = lin_queries[0].reshape(block_rows, q_heads, HEAD_SIZE).transpose(1, 0, 2)
    membrane_keys = lin_keys[0].reshape(block_rows, q_heads, HEAD_SIZE).transpose(1, 0, 2)
    cumulative = jnp.cumsum(decay_logs[0], axis=1)
    lower_mask = jnp.arange(block_rows)[:, None] >= jnp.arange(block_rows)[None, :]
    gaps = jnp.where(lower_mask[None], cumulative[:, :, None] - cumulative[:, None, :], 0.0)
    products = jnp.einsum(
        "hsd,htd->hst", membrane_queries, membrane_keys, preferred_element_type=jnp.float32
    )
    decayed = jnp.where(lower_mask[None], jnp.exp(gaps), 0.0) * products
    spike_float = spikes.astype(jnp.float32)
    query_float = membrane_queries.astype(jnp.float32)
    key_float = membrane_keys.astype(jnp.float32)
    block_decay = jnp.exp(cumulative[:, -1])
    tail_decay = jnp.exp(cumulative[:, -1:] - cumulative)
    local_state = jnp.einsum(
        "hsd,hse->hde", key_float * tail_decay[..., None], spike_float, precision=precise
    )
    identity = (jnp.ones_like(block_decay), jnp.zeros_like(local_state))
    decay_before, state_in = entering(
        (block_decay, local_state), "seq", chain_states, identity, False
    )
    carried = jnp.einsum("hsd,hde->hse", query_float, state_in, precision=precise)
    membrane = (
        jnp.einsum("hst,htd->hsd", decayed, spike_float, precision=precise)
        + jnp.exp(cumulative)[..., None] * carried
    )
    scale_out = 1.0 / jnp.sqrt(jnp.mean(membrane * membrane, axis=-1) + epsilon)
    unit_out = membrane * scale_out[..., None]
    layer_output = (
        unit_out.astype(jnp.bfloat16).transpose(1, 0, 2).reshape(1, block_rows, q_heads * HEAD_SIZE)
    )
    incoming = (
        cotangent[0].reshape(block_rows, q_heads, HEAD_SIZE).transpose(1, 0, 2).astype(jnp.float32)
    )
    membrane_grad = scale_out[..., None] * (
        incoming - unit_out * jnp.mean(incoming * unit_out, axis=-1, keepdims=True)
    )
    head_part = jnp.einsum(
        "hsd,hse->hde",
        query_float * jnp.exp(cumulative)[..., None],
        membrane_grad,
        precision=precise,
    )
    decay_after, state_after = entering(
        (block_decay, head_part), "seq", chain_states, identity, True
    )
    later_part = jnp.einsum("htd,hde->hte", key_float, state_after, precision=precise)
    spike_grad = (
        jnp.einsum("hst,hsd->htd", decayed, membrane_grad, precision=precise)
        + tail_decay[..., None] * later_part
    )
    level_grad = spike_grad * (1.0 - bounded * bounded)
    gain_part = jnp.sum(level_grad * normed, axis=1).reshape(q_heads * HEAD_SIZE)
    gain_grads = lax.psum(gain_part, ("seq", "dp"))
    normed_grad = level_grad * gain_rows
    slope_sum = lax.psum(jnp.sum(normed_grad * normed, axis=(0, 2)), "tensor")
    output_gradient = (
        inverse[None, :, None] * (normed_grad - normed * (slope_sum / D)[None, :, None])
    ).astype(jnp.bfloat16)

    def backward_head(operands):
        query_rows, grad_rows, row_max, row_sum, kv_index = operands
        key_row_block = lax.dynamic_index_in_dim(window_keys, kv_index, 0, keepdims=False)
        value_rows = lax.dynamic_index_in_dim(window_values, kv_index, 0, keepdims=False)
        key_reach = lax.dynamic_index_in_dim(key_window_length, kv_index, 0, keepdims=False)
        logits = head_logits(query_rows, key_row_block, first_query, key_reach, scaling)
        probs = jnp.exp(logits - row_max[:, None]) / row_sum[:, None]
        weights = probs.astype(jnp.bfloat16)
        prob_grad = jnp.einsum(
            "sd,kd->sk", grad_rows, value_rows, preferred_element_type=jnp.float32
        )
        row_delta = jnp.sum(probs * prob_grad, axis=-1, keepdims=True)
        logit_grad = (probs * (prob_grad - row_delta) * scaling).astype(jnp.bfloat16)
        query_grad = jnp.dot(logit_grad, key_row_block, preferred_element_type=jnp.float32)
        key_part = jnp.einsum(
            "sk,sd->kd", logit_grad, query_rows, preferred_element_type=jnp.float32
        )
        value_part = jnp.einsum("sk,sd->kd", weights, grad_rows, preferred_element_type=jnp.float32)
        return (query_grad, key_part, value_part)

    query_parts, key_parts, value_parts = lax.map(
        backward_head, (head_queries, output_gradient, maxima, sums, kv_of_head)
    )
    key_sum = key_parts.reshape(kv_heads, head_groups, key_span + block_rows, HEAD_SIZE).sum(axis=1)
    value_sum = value_parts.reshape(kv_heads, head_groups, key_span + block_rows, HEAD_SIZE).sum(
        axis=1
    )
    pair_grads = jnp.stack([key_sum, value_sum])
    own_grads = pair_grads[:, :, key_span:]
    carried_grads = jnp.zeros_like(own_grads)
    for distance in range(previous, 0, -1):
        offset = (previous - distance) * block_rows
        carried_grads = passed_along(
            carried_grads + pair_grads[:, :, offset : offset + block_rows], "seq", -1
        )
    total_grads = own_grads + carried_grads
    query_grads = (
        query_parts.astype(jnp.bfloat16)
        .transpose(1, 0, 2)
        .reshape(1, block_rows, q_heads * HEAD_SIZE)
    )
    key_gradient = (
        total_grads[0]
        .astype(jnp.bfloat16)
        .transpose(1, 0, 2)
        .reshape(1, block_rows, kv_heads * HEAD_SIZE)
    )
    value_gradient = (
        total_grads[1]
        .astype(jnp.bfloat16)
        .transpose(1, 0, 2)
        .reshape(1, block_rows, kv_heads * HEAD_SIZE)
    )
    return (layer_output, query_grads, key_gradient, value_gradient, gain_grads)


def solution(mesh):
    placed = (
        P("dp", "seq", "tensor"),
        P("dp", "seq", "tensor"),
        P("dp", "seq", "tensor"),
        P("tensor"),
        P("tensor"),
        P("tensor"),
        P("dp", "seq", "tensor"),
        P("dp", "seq", "tensor"),
        P("dp", "tensor", "seq"),
        P("dp", "seq", "tensor"),
    )
    return jax.shard_map(
        local,
        mesh=mesh,
        in_specs=placed,
        out_specs=(
            P("dp", "seq", "tensor"),
            P("dp", "seq", "tensor"),
            P("dp", "seq", "tensor"),
            P("dp", "seq", "tensor"),
            P("tensor"),
        ),
        check_vma=False,
    )
```

profile of v0, /device:TPU:1, one launch (start us, length us, event | category | flops | bytes accessed | tf_op | source)
XLA Modules:
  0.0 169.1 jit_solution(5383070077530054416)
XLA Ops:
  1.5 1.3 collective-permute-start
  3.5 1.1 copy.45
  4.6 1.1 copy.46
  6.0 1.1 convolution_multiply_fusion.3
  7.3 1.3 collective-permute-start.1
  9.2 1.2 collective-permute-done.1
  10.4 1.3 collective-permute-start.2
  11.7 1.3 convert_bitcast_fusion
  13.0 1.2 dynamic-slice
  15.2 3.8 %all-reduce = f32[14]{0:T(128)S(1)} all-reduce(f32[14]{0:T(128)S(1)} %dynamic-update-slice), channel_id=2, replica_groups=mesh['seq'=2,'dp'=4,'tensor'=4] {'seq'}, use_global_device_ids=true, to_apply=%add | all-reduce | flops 14 | bytes 112
  19.0 1.3 collective-permute-start.3
  21.9 1.1 copy.54
  26.5 33.9 %while.44 = (s32[]{:T(128)}, bf16[7,128,128]{2,1,0:T(8,128)(2,1)S(1)}, f32[7,128]{1,0:T(8,128)}, f32[7,128]{1,0:T(8,128)}, s32[]{:T(128)}, /*index=5*/s32[]{:T(1...) while((s32[]{:T(128)}, ...), condition=%wide.region_4.5_spmd, body=%wide.region_1.4_spmd.sunk | while | flops 42944384 | bytes 1389469 | solution.py:107
  27.2 1.1 fusion.113
  28.8 1.3 dynamic_update_slice.52
  30.1 1.3 dynamic_update_slice.51
  32.0 1.1 fusion.113
  33.6 1.3 dynamic_update_slice.52
  34.9 1.3 dynamic_update_slice.51
  36.9 1.1 fusion.113
  38.5 1.3 dynamic_update_slice.52
  39.8 1.3 dynamic_update_slice.51
  41.7 1.1 fusion.113
  43.3 1.3 dynamic_update_slice.52
  44.6 1.3 dynamic_update_slice.51
  46.6 1.1 fusion.113
  48.1 1.3 dynamic_update_slice.52
  49.4 1.3 dynamic_update_slice.51
  51.4 1.1 fusion.113
  53.0 1.3 dynamic_update_slice.52
  54.3 1.3 dynamic_update_slice.51
  56.2 1.1 fusion.113
  57.8 1.3 dynamic_update_slice.52
  59.1 1.3 dynamic_update_slice.51
  60.5 11.3 %psum.21 = f32[128]{0:T(128)} all-reduce(f32[128]{0:T(128)S(1)} %fusion.50), channel_id=1, replica_groups=mesh['seq'=2,'dp'=4,'tensor'=4] {'tensor'}, use_global_device_ids=true, to_apply=%region_6.7 | all-reduce | flops 128 | bytes 1024 | tf_op jit(solution)/shard_map/psum | solution.py:109
  72.5 1.5 fusion.62
  74.0 5.8 %all-gather.1 = f32[14,128,128]{2,1,0:T(8,128)S(1)} all-gather(f32[7,128,128]{2,1,0:T(8,128)S(1)} %fusion.62), channel_id=3, replica_groups=mesh['seq'=2,'dp'=4,'tensor'=4] {'seq'}, dimensions={0}, use_global_device_ids=true | all-gather | bytes 1376256 | tf_op jit(solution)/shard_map/all_gather | solution.py:25
  80.5 1.5 multiply_reduce_fusion.2
  82.1 1.1 fusion.59
  83.2 2.5 %all-gather.2 = f32[14,128,128]{2,1,0:T(8,128)S(1)} all-gather(f32[7,128,128]{2,1,0:T(8,128)S(1)} %fusion.59), channel_id=4, replica_groups=mesh['seq'=2,'dp'=4,'tensor'=4] {'seq'}, dimensions={0}, use_global_device_ids=true | all-gather | bytes 1376256 | tf_op jit(solution)/shard_map/all_gather | solution.py:25
  86.2 1.8 %fusion.49 = (f32[7,128]{1,0:T(8,128)S(1)}, f32[128]{0:T(128)S(1)}, f32[7,128,128]{2,1,0:T(8,128)}) fusion(bf16[7,128,128]{2,1,0:T(8,128)(2,1)S(1)} %get-tuple-element.348, f32[128]{0:T(128)S(1)} %add_rsqrt_fusion.1, f32[7,128]{1,0:T(8,128)S(1)} %bitcast.196, f32[7,128]{1,0:T(8,128)S(1)} %copy-done.14, f32[7,128,128]{2,1,0:T(8,128)S(1)} %fusion.38, ...), kind=kOutput, calls=%fused_computation.82 | convolution fusion | flops 178109440 | bytes 2542080 | tf_op jit(solution)/shard_map/hst,hsd->htd/dot_general | solution.py:164
  88.1 6.7 %psum.22 = f32[128]{0:T(128)S(1)} all-reduce(f32[128]{0:T(128)S(1)} %get-tuple-element.416), channel_id=1, replica_groups=mesh['seq'=2,'dp'=4,'tensor'=4] {'tensor'}, use_global_device_ids=true, to_apply=%region_10.11 | all-reduce | flops 128 | bytes 1024 | tf_op jit(solution)/shard_map/psum | solution.py:171
  94.7 1.2 fusion.48
  96.0 39.8 %while.45 = (s32[]{:T(128)}, bf16[7,128,128]{1,2,0:T(8,128)(2,1)}, f32[7,640,128]{2,1,0:T(8,128)}, f32[7,640,128]{2,1,0:T(8,128)S(1)}, s32[]{:T(128)}, /*index=5...) while((s32[]{:T(128)}, bf16[7,128,128]{1,2,0:T(8,128)(2,1)}, ...), condition=%wide.region_13.14_spmd, body=%wide.region_11.13_spmd.sunk | while | flops 106088448 | bytes 3815853 | solution.py:196
  97.6 1.1 multiply_reduce_fusion.4
  99.9 1.7 %fusion.127 = f32[7,640,128]{2,1,0:T(8,128)} fusion(f32[7,640,128]{2,1,0:T(8,128)} %get-tuple-element.702, s32[]{:T(128)S(6)} %copy.116, bf16[128,640]{1,0:T(8,128)(2,1)S(1)} %multiply_convert_fusion.5, bf16[7,128,128]{2,1,0:T(8,128)(2,1)} %get-tuple-element.721), kind=kOutput, calls=%fused_computation.26.clone.1 | convolution fusion | flops 20971520 | bytes 525312 | tf_op jit(solution)/shard_map/while/body/eval_jaxpr/sk,sd->kd/dot_general | solution.py:190
  103.2 1.1 multiply_reduce_fusion.4
  105.6 1.7 %fusion.127 = f32[7,640,128]{2,1,0:T(8,128)} fusion(f32[7,640,128]{2,1,0:T(8,128)} %get-tuple-element.702, s32[]{:T(128)S(6)} %copy.116, bf16[128,640]{1,0:T(8,128)(2,1)S(1)} %multiply_convert_fusion.5, bf16[7,128,128]{2,1,0:T(8,128)(2,1)} %get-tuple-element.721), kind=kOutput, calls=%fused_computation.26.clone.1 | convolution fusion | flops 20971520 | bytes 525312 | tf_op jit(solution)/shard_map/while/body/eval_jaxpr/sk,sd->kd/dot_general | solution.py:190
  108.9 1.1 multiply_reduce_fusion.4
  111.3 1.7 %fusion.127 = f32[7,640,128]{2,1,0:T(8,128)} fusion(f32[7,640,128]{2,1,0:T(8,128)} %get-tuple-element.702, s32[]{:T(128)S(6)} %copy.116, bf16[128,640]{1,0:T(8,128)(2,1)S(1)} %multiply_convert_fusion.5, bf16[7,128,128]{2,1,0:T(8,128)(2,1)} %get-tuple-element.721), kind=kOutput, calls=%fused_computation.26.clone.1 | convolution fusion | flops 20971520 | bytes 525312 | tf_op jit(solution)/shard_map/while/body/eval_jaxpr/sk,sd->kd/dot_general | solution.py:190
  114.6 1.1 multiply_reduce_fusion.4
  116.9 1.7 %fusion.127 = f32[7,640,128]{2,1,0:T(8,128)} fusion(f32[7,640,128]{2,1,0:T(8,128)} %get-tuple-element.702, s32[]{:T(128)S(6)} %copy.116, bf16[128,640]{1,0:T(8,128)(2,1)S(1)} %multiply_convert_fusion.5, bf16[7,128,128]{2,1,0:T(8,128)(2,1)} %get-tuple-element.721), kind=kOutput, calls=%fused_computation.26.clone.1 | convolution fusion | flops 20971520 | bytes 525312 | tf_op jit(solution)/shard_map/while/body/eval_jaxpr/sk,sd->kd/dot_general | solution.py:190
  120.3 1.1 multiply_reduce_fusion.4
  122.6 1.7 %fusion.127 = f32[7,640,128]{2,1,0:T(8,128)} fusion(f32[7,640,128]{2,1,0:T(8,128)} %get-tuple-element.702, s32[]{:T(128)S(6)} %copy.116, bf16[128,640]{1,0:T(8,128)(2,1)S(1)} %multiply_convert_fusion.5, bf16[7,128,128]{2,1,0:T(8,128)(2,1)} %get-tuple-element.721), kind=kOutput, calls=%fused_computation.26.clone.1 | convolution fusion | flops 20971520 | bytes 525312 | tf_op jit(solution)/shard_map/while/body/eval_jaxpr/sk,sd->kd/dot_general | solution.py:190
  126.0 1.1 multiply_reduce_fusion.4
  128.3 1.7 %fusion.127 = f32[7,640,128]{2,1,0:T(8,128)} fusion(f32[7,640,128]{2,1,0:T(8,128)} %get-tuple-element.702, s32[]{:T(128)S(6)} %copy.116, bf16[128,640]{1,0:T(8,128)(2,1)S(1)} %multiply_convert_fusion.5, bf16[7,128,128]{2,1,0:T(8,128)(2,1)} %get-tuple-element.721), kind=kOutput, calls=%fused_computation.26.clone.1 | convolution fusion | flops 20971520 | bytes 525312 | tf_op jit(solution)/shard_map/while/body/eval_jaxpr/sk,sd->kd/dot_general | solution.py:190
  131.6 1.1 multiply_reduce_fusion.4
  134.0 1.7 %fusion.127 = f32[7,640,128]{2,1,0:T(8,128)} fusion(f32[7,640,128]{2,1,0:T(8,128)} %get-tuple-element.702, s32[]{:T(128)S(6)} %copy.116, bf16[128,640]{1,0:T(8,128)(2,1)S(1)} %multiply_convert_fusion.5, bf16[7,128,128]{2,1,0:T(8,128)(2,1)} %get-tuple-element.721), kind=kOutput, calls=%fused_computation.26.clone.1 | convolution fusion | flops 20971520 | bytes 525312 | tf_op jit(solution)/shard_map/while/body/eval_jaxpr/sk,sd->kd/dot_general | solution.py:190
  135.9 1.8 %reduce_sum.91 = f32[640,128]{1,0:T(8,128)S(1)} reduce(f32[7,640,128]{2,1,0:T(8,128)} %get-tuple-element.352, f32[]{:T(128)} %constant.152.clone.1), dimensions={0}, to_apply=%region_14.15 | reduce | flops 491520 | bytes 2621444 | tf_op jit(solution)/shard_map/reduce_sum | solution.py:199
  137.7 4.1 %collective-permute-start.4 = (f32[2,1,128,128]{3,2,1,0:T(8,128)S(1)}, f32[2,1,128,128]{3,2,1,0:T(8,128)S(1)}, u32[]{:S(2)}, u32[]{:S(2)}) collective-permute-start(f32[2,1,128,128]{3,2,1,0:T(8,128)S(1)} %fusion.78), channel_id=1, source_target_pairs={{16,0},{17,1},{18,2},{19,3},{20,4},{21,5},{22,6},{23,7},{24,8},{25... | collective-permute-start | bytes 393224 | tf_op jit(solution)/shard_map/ppermute | solution.py:20
  142.8 2.3 %collective-permute-start.5 = (f32[2,1,128,128]{3,2,1,0:T(8,128)S(1)}, f32[2,1,128,128]{3,2,1,0:T(8,128)S(1)}, u32[]{:S(2)}, u32[]{:S(2)}) collective-permute-start(f32[2,1,128,128]{3,2,1,0:T(8,128)S(1)} %fusion.80), channel_id=1, source_target_pairs={{16,0},{17,1},{18,2},{19,3},{20,4},{21,5},{22,6},{23,7},{24,8},{25... | collective-permute-start | bytes 393224 | tf_op jit(solution)/shard_map/ppermute | solution.py:20
  146.0 2.3 %collective-permute-start.6 = (f32[2,1,128,128]{3,2,1,0:T(8,128)S(1)}, f32[2,1,128,128]{3,2,1,0:T(8,128)S(1)}, u32[]{:S(2)}, u32[]{:S(2)}) collective-permute-start(f32[2,1,128,128]{3,2,1,0:T(8,128)S(1)} %fusion.74), channel_id=1, source_target_pairs={{16,0},{17,1},{18,2},{19,3},{20,4},{21,5},{22,6},{23,7},{24,8},{25... | collective-permute-start | bytes 393224 | tf_op jit(solution)/shard_map/ppermute | solution.py:20
  149.3 2.3 %collective-permute-start.7 = (f32[2,1,128,128]{3,2,1,0:T(8,128)S(1)}, f32[2,1,128,128]{3,2,1,0:T(8,128)S(1)}, u32[]{:S(2)}, u32[]{:S(2)}) collective-permute-start(f32[2,1,128,128]{3,2,1,0:T(8,128)S(1)} %fusion.81), channel_id=1, source_target_pairs={{16,0},{17,1},{18,2},{19,3},{20,4},{21,5},{22,6},{23,7},{24,8},{25... | collective-permute-start | bytes 393224 | tf_op jit(solution)/shard_map/ppermute | solution.py:20
  153.3 15.1 %psum.23 = f32[896]{0:T(1024)} all-reduce(f32[896]{0:T(1024)S(1)} %bitcast.198), channel_id=1, replica_groups=mesh['seq'=2,'dp'=4,'tensor'=4] {'seq','dp'}, use_global_device_ids=true, to_apply=%region_17.18 | all-reduce | flops 896 | bytes 7168 | tf_op jit(solution)/shard_map/psum | solution.py:169
  (177 shorter events, 43.0 us)
Async XLA Ops:
  0.6 25.8 %copy-start.7 = (bf16[1,128,128]{2,1,0:T(8,128)(2,1)S(1)}, bf16[1,128,128]{2,1,0:T(8,128)(2,1)}, u32[]{:S(2)}) copy-start(bf16[1,128,128]{2,1,0:T(8,128)(2,1)} %param.16) | copy-start | bytes 98308
  0.6 25.8 %copy-start.8 = (bf16[1,128,128]{2,1,0:T(8,128)(2,1)S(1)}, bf16[1,128,128]{2,1,0:T(8,128)(2,1)}, u32[]{:S(2)}) copy-start(bf16[1,128,128]{2,1,0:T(8,128)(2,1)} %param.15) | copy-start | bytes 98308
  0.7 20.3 %copy-start.5 = (bf16[1,128,896]{2,1,0:T(8,128)(2,1)S(1)}, bf16[1,128,896]{2,1,0:T(8,128)(2,1)}, u32[]{:S(2)}) copy-start(bf16[1,128,896]{2,1,0:T(8,128)(2,1)} %param.14) | copy-start | bytes 688132
  1.5 5.8 %collective-permute-start = (bf16[2,1,128,128]{3,2,1,0:T(8,128)(2,1)S(1)}, bf16[2,1,128,128]{3,2,1,0:T(8,128)(2,1)S(1)}, u32[]{:S(2)}, u32[]{:S(2)}) collective-permute-start(bf16[2,1,128,128]{3,2,1,0:T(8,128)(2,1)S(1)} %pad_maximum_fusion.1), channel_id=1, source_target_pairs={{0,16},{1,17},{2,18},{3,19},{4,20},{5,21},{6,22},{7,23},{8,24},{9,... | collective-permute-start | bytes 196616 | tf_op jit(solution)/shard_map/ppermute | solution.py:20
  5.7 15.2 %copy-start.2 = (bf16[1,128,896]{1,2,0:T(8,128)(2,1)}, bf16[1,128,896]{1,2,0:T(8,128)(2,1)S(1)}, u32[]{:S(2)}) copy-start(bf16[1,128,896]{1,2,0:T(8,128)(2,1)S(1)} %copy.46) | copy-start | bytes 688132
  7.3 13.6 %copy-start.9 = (bf16[2,1,128,128]{3,2,1,0:T(8,128)(2,1)}, bf16[2,1,128,128]{3,2,1,0:T(8,128)(2,1)S(1)}, u32[]{:S(2)}) copy-start(bf16[2,1,128,128]{3,2,1,0:T(8,128)(2,1)S(1)} %collective-permute-done) | copy-start | bytes 196612
  7.3 3.1 %collective-permute-start.1 = (bf16[2,1,128,128]{3,2,1,0:T(8,128)(2,1)S(1)}, bf16[2,1,128,128]{3,2,1,0:T(8,128)(2,1)S(1)}, u32[]{:S(2)}, u32[]{:S(2)}) collective-permute-start(bf16[2,1,128,128]{3,2,1,0:T(8,128)(2,1)S(1)} %collective-permute-done), channel_id=1, source_target_pairs={{0,16},{1,17},{2,18},{3,19},{4,20},{5,21},{6,22},{7,23},{8,24},{9,... | collective-permute-start | bytes 196616 | tf_op jit(solution)/shard_map/ppermute | solution.py:20
  10.4 10.4 %copy-start.10 = (bf16[2,1,128,128]{3,2,1,0:T(8,128)(2,1)}, bf16[2,1,128,128]{3,2,1,0:T(8,128)(2,1)S(1)}, u32[]{:S(2)}) copy-start(bf16[2,1,128,128]{3,2,1,0:T(8,128)(2,1)S(1)} %collective-permute-done.1) | copy-start | bytes 196612
  10.4 8.5 %collective-permute-start.2 = (bf16[2,1,128,128]{3,2,1,0:T(8,128)(2,1)S(1)}, bf16[2,1,128,128]{3,2,1,0:T(8,128)(2,1)}, u32[]{:S(2)}, u32[]{:S(2)}) collective-permute-start(bf16[2,1,128,128]{3,2,1,0:T(8,128)(2,1)S(1)} %collective-permute-done.1), channel_id=1, source_target_pairs={{0,16},{1,17},{2,18},{3,19},{4,20},{5,21},{6,22},{7,23},{8,24},{9,... | collective-permute-start | bytes 196616 | tf_op jit(solution)/shard_map/ppermute | solution.py:20
  19.0 4.0 %collective-permute-start.3 = (bf16[2,1,128,128]{3,2,1,0:T(8,128)(2,1)}, bf16[2,1,128,128]{3,2,1,0:T(8,128)(2,1)}, u32[]{:S(2)}, u32[]{:S(2)}) collective-permute-start(bf16[2,1,128,128]{3,2,1,0:T(8,128)(2,1)} %collective-permute-done.2), channel_id=1, source_target_pairs={{0,16},{1,17},{2,18},{3,19},{4,20},{5,21},{6,22},{7,23},{8,24},{9,... | collective-permute-start | bytes 196616 | tf_op jit(solution)/shard_map/ppermute | solution.py:20
  60.4 19.4 %copy-start.16 = (f32[7]{0:T(128)S(1)}, f32[7]{0:T(128)}, u32[]{:S(2)}) copy-start(f32[7]{0:T(128)} %get-tuple-element.487) | copy-start | bytes 88
  72.4 13.8 %copy-start.17 = (f32[128]{0:T(128)}, f32[128]{0:T(128)S(1)}, u32[]{:S(2)}) copy-start(f32[128]{0:T(128)S(1)} %add_rsqrt_fusion.1) | copy-start | bytes 1540
  72.4 8.0 %copy-start.11 = (f32[7,128]{1,0:T(8,128)S(1)}, f32[7,128]{1,0:T(8,128)}, u32[]{:S(2)}) copy-start(f32[7,128]{1,0:T(8,128)} %get-tuple-element.484) | copy-start | bytes 10756
  72.4 8.0 %copy-start.12 = (f32[896]{0:T(1024)S(1)}, f32[896]{0:T(1024)}, u32[]{:S(2)}) copy-start(f32[896]{0:T(1024)} %param.18) | copy-start | bytes 10756
  72.4 8.1 %copy-start.14 = (f32[7,128]{1,0:T(8,128)S(1)}, f32[7,128]{1,0:T(8,128)}, u32[]{:S(2)}) copy-start(f32[7,128]{1,0:T(8,128)} %convert_bitcast_fusion) | copy-start | bytes 10756
  72.4 8.0 %copy-start.18 = (f32[7,128,128]{2,1,0:T(8,128)S(1)}, f32[7,128,128]{2,1,0:T(8,128)}, u32[]{:S(2)}) copy-start(f32[7,128,128]{2,1,0:T(8,128)} %convolution_multiply_fusion.3) | copy-start | bytes 1376260
  80.5 2.8 %copy-start = (f32[7,128,128]{2,1,0:T(8,128)}, f32[7,128,128]{2,1,0:T(8,128)S(1)}, u32[]{:S(2)}) copy-start(f32[7,128,128]{2,1,0:T(8,128)S(1)} %fusion.54) | copy-start | bytes 1376260
  82.0 3.7 %copy-start.3 = (bf16[1,128,896]{1,2,0:T(8,128)(2,1)S(1)}, bf16[1,128,896]{1,2,0:T(8,128)(2,1)}, u32[]{:S(2)}) copy-start(bf16[1,128,896]{1,2,0:T(8,128)(2,1)} %copy-done.2) | copy-start | bytes 688132
  82.0 3.7 %copy-start.15 = (f32[7]{0:T(128)S(1)}, f32[7]{0:T(128)}, u32[]{:S(2)}) copy-start(f32[7]{0:T(128)} %get-tuple-element.486) | copy-start | bytes 88
  85.7 9.0 %copy-start.13 = (f32[896]{0:T(1024)S(1)}, f32[896]{0:T(1024)}, u32[]{:S(2)}) copy-start(f32[896]{0:T(1024)} %param.18) | copy-start | bytes 10756
  137.7 13.9 %copy-start.1 = (f32[7,128,128]{2,1,0:T(8,128)S(1)}, f32[7,128,128]{2,1,0:T(8,128)}, u32[]{:S(2)}) copy-start(f32[7,128,128]{2,1,0:T(8,128)} %copy-done) | copy-start | bytes 1376260
  137.7 13.9 %copy-start.4 = (f32[7,128,128]{1,2,0:T(8,128)S(1)}, f32[7,128,128]{1,2,0:T(8,128)}, u32[]{:S(2)}) copy-start(f32[7,128,128]{1,2,0:T(8,128)} %get-tuple-element.488) | copy-start | bytes 1376260
  137.7 14.8 %copy-start.6 = (bf16[7,128,128]{1,2,0:T(8,128)(2,1)S(1)}, bf16[7,128,128]{1,2,0:T(8,128)(2,1)}, u32[]{:S(2)}) copy-start(bf16[7,128,128]{1,2,0:T(8,128)(2,1)} %get-tuple-element.351) | copy-start | bytes 688132
  137.7 5.0 %collective-permute-start.4 = (f32[2,1,128,128]{3,2,1,0:T(8,128)S(1)}, f32[2,1,128,128]{3,2,1,0:T(8,128)S(1)}, u32[]{:S(2)}, u32[]{:S(2)}) collective-permute-start(f32[2,1,128,128]{3,2,1,0:T(8,128)S(1)} %fusion.78), channel_id=1, source_target_pairs={{16,0},{17,1},{18,2},{19,3},{20,4},{21,5},{22,6},{23,7},{24,8},{25... | collective-permute-start | bytes 393224 | tf_op jit(solution)/shard_map/ppermute | solution.py:20
  142.8 3.2 %collective-permute-start.5 = (f32[2,1,128,128]{3,2,1,0:T(8,128)S(1)}, f32[2,1,128,128]{3,2,1,0:T(8,128)S(1)}, u32[]{:S(2)}, u32[]{:S(2)}) collective-permute-start(f32[2,1,128,128]{3,2,1,0:T(8,128)S(1)} %fusion.80), channel_id=1, source_target_pairs={{16,0},{17,1},{18,2},{19,3},{20,4},{21,5},{22,6},{23,7},{24,8},{25... | collective-permute-start | bytes 393224 | tf_op jit(solution)/shard_map/ppermute | solution.py:20
  146.0 3.2 %collective-permute-start.6 = (f32[2,1,128,128]{3,2,1,0:T(8,128)S(1)}, f32[2,1,128,128]{3,2,1,0:T(8,128)S(1)}, u32[]{:S(2)}, u32[]{:S(2)}) collective-permute-start(f32[2,1,128,128]{3,2,1,0:T(8,128)S(1)} %fusion.74), channel_id=1, source_target_pairs={{16,0},{17,1},{18,2},{19,3},{20,4},{21,5},{22,6},{23,7},{24,8},{25... | collective-permute-start | bytes 393224 | tf_op jit(solution)/shard_map/ppermute | solution.py:20
  149.3 19.1 %collective-permute-start.7 = (f32[2,1,128,128]{3,2,1,0:T(8,128)S(1)}, f32[2,1,128,128]{3,2,1,0:T(8,128)S(1)}, u32[]{:S(2)}, u32[]{:S(2)}) collective-permute-start(f32[2,1,128,128]{3,2,1,0:T(8,128)S(1)} %fusion.81), channel_id=1, source_target_pairs={{16,0},{17,1},{18,2},{19,3},{20,4},{21,5},{22,6},{23,7},{24,8},{25... | collective-permute-start | bytes 393224 | tf_op jit(solution)/shard_map/ppermute | solution.py:20
where the time goes:
time: 172 us; the launch traced here: 169 us
  matrix products  46.9 us (27%)
  blocking collectives  45.2 us (26%)
  local copies, waits for them, and re-layouts  35.5 us (21%)
  other arithmetic  19.2 us (11%)
  starting transfers between devices  16 us (9%)
  waiting for transfers between devices  4.14 us (2%)
  between operations  1.74 us (1%)
    dynamic_update_slice x14, local copies, waits for them, and re-layouts, local(): heads_out, maxima, sums = lax.map(forward_head, (head_queries, kv_of_head))  18.1 us
    ppermute x8, starting transfers between devices, passed_along(): return lax.ppermute(block, axis, route)  16 us
    dot_general x14, matrix products, head_logits(): jnp.einsum('sd,kd->sk', query_rows, key_row_block, preferred_element_type...  15.4 us
    psum x1, blocking collectives, local(): gain_grads = lax.psum(gain_part, ('seq', 'dp'))  15.1 us
    dot_general x7, matrix products, backward_head(): jnp.einsum('sk,sd->kd', logit_grad, query_rows, preferred_element_type=jn...  12.1 us
    psum x1, blocking collectives, local(): square_sum = lax.psum(jnp.sum(out_float * out_float, axis=(0, 2)), 'tensor')  11.3 us
    unnamed x51, local copies, waits for them, and re-layouts  9.7 us
    add x14, other arithmetic, head_logits(): query_pos = first_query + jnp.arange(block_rows, dtype=jnp.int32)[:, None]  9.07 us
  transfers between devices with their start and end apart: 8, of which 4 were waited for; matrix products, arithmetic and copies ran while one was open for 7% of the time, Pallas kernels for 0%

commit v1 on v0

v1 whole, which is shorter than its diff:
```python
import functools
import math

import jax
import jax.numpy as jnp
from jax import lax
from jax.experimental import pallas as pl
from jax.experimental.pallas import tpu as pltpu
from jax.sharding import PartitionSpec as P

HEAD_SIZE = 128
D = 3584
LONGEST_WINDOW = 512

MESH = pl.DeviceIdType.MESH
f32 = jnp.float32
bf16 = jnp.bfloat16
precise = lax.Precision.HIGHEST
epsilon = 1e-06


def nn(left, right):
    return lax.dot_general(left, right, (((1,), (0,)), ((), ())), preferred_element_type=f32)


def nt(left, right):
    return lax.dot_general(left, right, (((1,), (1,)), ((), ())), preferred_element_type=f32)


def turned(block):
    return block.astype(f32).T


def kernel(
    sizes,
    q_ref,
    k_ref,
    v_ref,
    window_ref,
    gain_ref,
    level_ref,
    lq_ref,
    lk_ref,
    decay_ref,
    ct_ref,
    out_ref,
    qg_ref,
    kg_ref,
    vg_ref,
    gg_ref,
    pair_prev,
    probs,
    heads_out,
    decayed,
    ct_turned,
    gain_cols,
    level_cols,
    bounded_buf,
    spikes_buf,
    work,
    out_grads,
    logit_grads,
    weights_buf,
    part_one,
    part_two,
    square_slots,
    slope_slots,
    state_out,
    state_in,
    after_out,
    after_in,
    gain_slots,
    gain_sum_slots,
    pair_out,
    pair_in,
    pair_send,
    pair_recv,
    square_send,
    square_recv,
    state_send,
    state_recv,
    after_send,
    after_recv,
    slope_send,
    slope_recv,
    dp_send,
    dp_recv,
    seq_send,
    seq_recv,
    grad_send,
    grad_recv,
):
    n_seq, n_dp, n_tensor, previous, heads = sizes
    seq, dp, ten = lax.axis_index("seq"), lax.axis_index("dp"), lax.axis_index("tensor")
    size = HEAD_SIZE
    scaling = 1.0 / math.sqrt(HEAD_SIZE)
    cols = [slice(h * size, (h + 1) * size) for h in range(heads)]

    barrier = pltpu.get_barrier_semaphore()
    for axis, me, count in (("seq", seq, n_seq), ("dp", dp, n_dp), ("tensor", ten, n_tensor)):
        for step in range(1, count):
            pl.semaphore_signal(
                barrier,
                inc=1,
                device_id={axis: lax.rem(me + step, count)},
                device_id_type=MESH,
            )
    pl.semaphore_wait(barrier, n_seq + n_dp + n_tensor - 3)

    def remote(src, dst, send, recv, axis, target):
        return pltpu.make_async_remote_copy(
            src_ref=src,
            dst_ref=dst,
            send_sem=send,
            recv_sem=recv,
            device_id={axis: target},
            device_id_type=MESH,
        )

    def exchange(slots, send, recv, axis, me, count):
        def start():
            for step in range(1, count):
                remote(
                    slots.at[me],
                    slots.at[me],
                    send.at[step - 1],
                    recv.at[me],
                    axis,
                    lax.rem(me + step, count),
                ).start()

        def wait():
            for step in range(1, count):
                sender = lax.rem(me + count - step, count)
                copy = remote(
                    slots.at[me], slots.at[sender], send.at[step - 1], recv.at[sender], axis, sender
                )
                copy.wait_recv()

        def drain():
            for step in range(1, count):
                remote(
                    slots.at[me],
                    slots.at[me],
                    send.at[step - 1],
                    recv.at[me],
                    axis,
                    lax.rem(me + step, count),
                ).wait_send()

        return start, wait, drain

    def pair_copy(index, distance):
        source = (k_ref, v_ref)[index].at[0]
        return remote(
            source,
            pair_prev.at[index, distance - 1],
            pair_send.at[index, distance - 1],
            pair_recv.at[index, distance - 1],
            "seq",
            lax.rem(seq + distance, n_seq),
        )

    def grad_copy(index, distance):
        return remote(
            pair_out.at[index, distance - 1],
            pair_in.at[index, distance - 1],
            grad_send.at[index, distance - 1],
            grad_recv.at[index, distance - 1],
            "seq",
            lax.rem(seq + n_seq - distance, n_seq),
        )

    for distance in range(1, previous + 1):

        @pl.when(seq + distance < n_seq)
        def _():
            pair_copy(0, distance).start()
            pair_copy(1, distance).start()

        @pl.when(seq < distance)
        def _():
            for index in range(2):
                pair_prev[index, distance - 1] = jnp.zeros((size, size), bf16)

    row_index = lax.broadcasted_iota(jnp.int32, (size, size), 0)
    column_index = lax.broadcasted_iota(jnp.int32, (size, size), 1)
    causal = row_index <= column_index
    window = window_ref[0]
    keys = k_ref[0]
    values = v_ref[0]
    keys_turned = turned(keys).astype(bf16)
    values_turned = turned(values).astype(bf16)

    for h in range(heads):
        scores = nt(keys, q_ref[0, :, cols[h]]) * scaling
        probs[0, h] = jnp.where(causal, scores, -jnp.inf)

    def attend(blocks):
        squares = jnp.zeros((size, size), f32)
        block_keys = [pair_prev[0, d] for d in range(blocks)]
        block_values = [turned(pair_prev[1, d]).astype(bf16) for d in range(blocks)]
        masks = []
        for d in range(blocks):
            seen = (d + 1) * size + column_index - row_index < window
            masks.append(seen & (seq > d) if n_seq > 2 else seen)
        for h in range(heads):
            scores = [probs[0, h]]
            for d in range(blocks):
                score = nt(block_keys[d], q_ref[0, :, cols[h]]) * scaling
                scores.append(jnp.where(masks[d], score, -jnp.inf))
            top = functools.reduce(
                jnp.maximum, [jnp.max(score, axis=0, keepdims=True) for score in scores]
            )
            exponents = [jnp.exp(score - top) for score in scores]
            total = sum(jnp.sum(exponent, axis=0, keepdims=True) for exponent in exponents)
            share = 1.0 / total
            result = None
            for d, exponent in enumerate(exponents):
                prob = exponent * share
                probs[d, h] = prob
                weights = prob.astype(bf16)
                weights_buf[d, :, cols[h]] = weights
                part = nn(values_turned if d == 0 else block_values[d - 1], weights)
                result = part if result is None else result + part
            result = result.astype(bf16).astype(f32)
            heads_out[h] = result
            squares = squares + result * result
        part_one[...] = jnp.broadcast_to(jnp.sum(squares, axis=0, keepdims=True), (8, size))

    @pl.when(seq == 0)
    def _():
        attend(0)

    if previous:

        @pl.when(seq > 0)
        def _():
            for distance in range(1, previous + 1):

                @pl.when(seq >= distance)
                def _():
                    pair_copy(0, distance).wait_recv()
                    pair_copy(1, distance).wait_recv()

            attend(previous)

    square_slots[ten] = part_one[...]
    start, wait_squares, drain_squares = exchange(
        square_slots, square_send, square_recv, "tensor", ten, n_tensor
    )
    start()

    logs = decay_ref[0]
    upper = jnp.where(causal, 1.0, 0.0)
    cumulative = jnp.dot(logs, upper, precision=precise, preferred_element_type=f32)
    whole = jnp.dot(
        logs, jnp.ones((size, size), f32), precision=precise, preferred_element_type=f32
    )
    tail = jnp.exp(jnp.minimum(whole - cumulative, 0.0))
    grown = jnp.exp(cumulative)
    block_decay = jnp.exp(whole)
    for h in range(heads):
        level_rows = jnp.broadcast_to(level_ref[h : h + 1, :].astype(f32), (size, size))
        gain_rows = jnp.broadcast_to(gain_ref[h : h + 1, :], (size, size))
        level_cols[h] = level_rows.T
        gain_cols[h] = gain_rows.T
        ct_turned[h] = turned(ct_ref[0, :, cols[h]])
        along = jnp.broadcast_to(cumulative[h : h + 1, :], (size, size))
        gaps = jnp.where(causal, along - along.T, -jnp.inf)
        product = nt(lk_ref[0, :, cols[h]], lq_ref[0, :, cols[h]])
        decayed[h] = (jnp.exp(gaps) * product).astype(bf16)

    wait_squares()
    square_sum = sum(square_slots[i] for i in range(n_tensor))[:1]
    inverse = 1.0 / jnp.sqrt(square_sum / D + epsilon)

    def state_copy(h):
        return remote(
            state_out.at[h],
            state_in.at[h],
            state_send.at[h],
            state_recv.at[h],
            "seq",
            lax.rem(seq + 1, n_seq),
        )

    def after_copy(h):
        return remote(
            after_out.at[h],
            after_in.at[h],
            after_send.at[h],
            after_recv.at[h],
            "seq",
            lax.rem(seq + n_seq - 1, n_seq),
        )

    for h in range(heads):
        normed = heads_out[h] * inverse
        heads_out[h] = normed
        bounded = jnp.tanh(normed * gain_cols[h] / level_cols[h])
        bounded_buf[h] = bounded
        spikes = (level_cols[h] * bounded).astype(bf16)
        spikes_buf[h] = spikes
        fading = (spikes.astype(f32) * tail[h : h + 1]).astype(bf16)
        state_out[h] = nn(fading, lk_ref[0, :, cols[h]]).astype(state_out.dtype)
        if n_seq == 2:

            @pl.when(seq == 0)
            def _():
                state_copy(h).start()

    for h in range(heads):
        work[h] = nn(spikes_buf[h], decayed[h])

    if n_seq > 2:

        @pl.when(seq == 0)
        def _():
            for h in range(heads):
                state_copy(h).start()

    if n_seq > 1:

        @pl.when(seq > 0)
        def _():
            for h in range(heads):
                state_copy(h).wait_recv()
                if n_seq > 2:
                    state_out[h] = (
                        block_decay[h : h + 1] * state_in[h].astype(f32) + state_out[h].astype(f32)
                    ).astype(state_out.dtype)

                    @pl.when(seq < n_seq - 1)
                    def _():
                        state_copy(h).start()

            for h in range(heads):
                carried = nt(state_in[h].astype(bf16), lq_ref[0, :, cols[h]])
                work[h] = work[h] + grown[h : h + 1] * carried

    for h in range(heads):
        membrane = work[h]
        mean = jnp.sum(membrane * membrane, axis=0, keepdims=True) / size
        scale = 1.0 / jnp.sqrt(mean + epsilon)
        unit = membrane * scale
        incoming = ct_turned[h]
        inner = jnp.sum(incoming * unit, axis=0, keepdims=True) / size
        grad = scale * (incoming - unit * inner)
        work[h] = unit
        spikes_buf[h] = grad.astype(bf16)
        after_out[h] = nn((grad * grown[h : h + 1]).astype(bf16), lq_ref[0, :, cols[h]]).astype(
            after_out.dtype
        )
        if n_seq == 2:

            @pl.when(seq == 1)
            def _():
                after_copy(h).start()

    if n_seq > 2:

        @pl.when(seq == n_seq - 1)
        def _():
            for h in range(heads):
                after_copy(h).start()

    for h in range(heads):
        out_ref[0, :, cols[h]] = work[h].T.astype(bf16)
        work[h] = nt(spikes_buf[h], decayed[h])

    if n_seq > 1:

        @pl.when(seq < n_seq - 1)
        def _():
            for h in range(heads):
                after_copy(h).wait_recv()
                if n_seq > 2:
                    after_out[h] = (
                        block_decay[h : h + 1] * after_in[h].astype(f32) + after_out[h].astype(f32)
                    ).astype(after_out.dtype)

                    @pl.when(seq > 0)
                    def _():
                        after_copy(h).start()

            for h in range(heads):
                later = nt(after_in[h].astype(bf16), lk_ref[0, :, cols[h]])
                work[h] = work[h] + tail[h : h + 1] * later

    slope_part = jnp.zeros((size, size), f32)
    for h in range(heads):
        bounded = bounded_buf[h]
        level_grad = work[h] * (1.0 - bounded * bounded)
        with_normed = level_grad * heads_out[h]
        work[h] = level_grad
        bounded_buf[h] = with_normed
        slope_part = slope_part + with_normed * gain_cols[h]
    part_two[...] = jnp.broadcast_to(jnp.sum(slope_part, axis=0, keepdims=True), (8, size))
    slope_slots[ten] = part_two[...]
    start, wait_slopes, drain_slopes = exchange(
        slope_slots, slope_send, slope_recv, "tensor", ten, n_tensor
    )
    start()

    rows = [jnp.sum(bounded_buf[h].T, axis=0, keepdims=True) for h in range(heads)]
    rows.append(jnp.zeros((8 - heads, size), f32))
    gain_slots[dp] = jnp.concatenate(rows, axis=0)
    start, wait_dp, drain_dp = exchange(gain_slots, dp_send, dp_recv, "dp", dp, n_dp)
    start()

    wait_slopes()
    slope = sum(slope_slots[i] for i in range(n_tensor))[:1] / D
    for h in range(heads):
        normed_grad = work[h] * gain_cols[h]
        out_grads[:, cols[h]] = (inverse * (normed_grad - heads_out[h] * slope)).astype(bf16)

    def back(blocks):
        block_values = [values] + [pair_prev[1, d] for d in range(blocks)]
        for h in range(heads):
            prob_grads = [nn(block, out_grads[:, cols[h]]) for block in block_values]
            delta = sum(
                jnp.sum(probs[d, h] * prob_grad, axis=0, keepdims=True)
                for d, prob_grad in enumerate(prob_grads)
            )
            for d, prob_grad in enumerate(prob_grads):
                logit_grad = probs[d, h] * (prob_grad - delta) * scaling
                logit_grads[d, :, cols[h]] = logit_grad.astype(bf16)

    def pair_sums(d):
        key_sum = sum(nn(logit_grads[d, :, cols[h]], q_ref[0, :, cols[h]]) for h in range(heads))
        value_sum = nt(weights_buf[d], out_grads[...])
        return key_sum, value_sum

    @pl.when(seq == 0)
    def _():
        back(0)

    if previous:

        @pl.when(seq > 0)
        def _():
            back(previous)
            for distance in range(1, previous + 1):
                key_sum, value_sum = pair_sums(distance)
                pair_out[0, distance - 1] = key_sum
                pair_out[1, distance - 1] = value_sum

                @pl.when(seq >= distance)
                def _():
                    grad_copy(0, distance).start()
                    grad_copy(1, distance).start()

    wait_dp()
    gain_sum_slots[seq] = sum(gain_slots[i] for i in range(n_dp))
    start, wait_seq, drain_seq = exchange(gain_sum_slots, seq_send, seq_recv, "seq", seq, n_seq)
    start()

    @pl.when(seq == 0)
    def _():
        for h in range(heads):
            query_grad = nn(keys_turned, logit_grads[0, :, cols[h]])
            qg_ref[0, :, cols[h]] = query_grad.T.astype(bf16)

    if previous:

        @pl.when(seq > 0)
        def _():
            earlier = [turned(pair_prev[0, d]).astype(bf16) for d in range(previous)]
            for h in range(heads):
                query_grad = nn(keys_turned, logit_grads[0, :, cols[h]])
                for d in range(previous):
                    query_grad = query_grad + nn(earlier[d], logit_grads[d + 1, :, cols[h]])
                qg_ref[0, :, cols[h]] = query_grad.T.astype(bf16)

    key_sum, value_sum = pair_sums(0)
    pair_out[0, previous] = key_sum
    pair_out[1, previous] = value_sum
    wait_seq()
    gg_ref[...] = sum(gain_sum_slots[i] for i in range(n_seq))[:heads]

    for distance in range(1, previous + 1):

        @pl.when(seq + distance < n_seq)
        def _():
            for index in range(2):
                grad_copy(index, distance).wait_recv()
                pair_out[index, previous] = (
                    pair_out[index, previous] + pair_in[index, distance - 1]
                )

    kg_ref[0] = pair_out[0, previous].astype(bf16)
    vg_ref[0] = pair_out[1, previous].astype(bf16)

    for distance in range(1, previous + 1):

        @pl.when(seq + distance < n_seq)
        def _():
            pair_copy(0, distance).wait_send()
            pair_copy(1, distance).wait_send()

        @pl.when(seq >= distance)
        def _():
            grad_copy(0, distance).wait_send()
            grad_copy(1, distance).wait_send()

    if n_seq > 1:

        @pl.when(seq < n_seq - 1)
        def _():
            for h in range(heads):
                state_copy(h).wait_send()

        @pl.when(seq > 0)
        def _():
            for h in range(heads):
                after_copy(h).wait_send()

    drain_squares()
    drain_slopes()
    drain_dp()
    drain_seq()


def local(
    attention_queries,
    attention_keys,
    attention_values,
    key_window_length,
    norm_gain,
    spike_levels,
    lin_queries,
    lin_keys,
    decay_logs,
    cotangent,
):
    n_seq, n_dp, n_tensor = (lax.axis_size(axis) for axis in ("seq", "dp", "tensor"))
    rows = attention_queries.shape[1]
    heads = attention_queries.shape[2] // HEAD_SIZE
    previous = min((LONGEST_WINDOW + rows - 1) // rows, n_seq - 1)
    slots = max(previous, 1)
    state_type = bf16 if n_seq == 2 else f32
    size = HEAD_SIZE
    vmem = pl.BlockSpec(memory_space=pltpu.VMEM)
    smem = pl.BlockSpec(memory_space=pltpu.SMEM)
    tiles = (heads, size, size)
    dma = pltpu.SemaphoreType.DMA
    outputs = (
        jax.ShapeDtypeStruct(attention_queries.shape, bf16),
        jax.ShapeDtypeStruct(attention_queries.shape, bf16),
        jax.ShapeDtypeStruct(attention_keys.shape, bf16),
        jax.ShapeDtypeStruct(attention_keys.shape, bf16),
        jax.ShapeDtypeStruct((heads, size), f32),
    )
    scratch = [
        pltpu.VMEM((2, slots, size, size), bf16),
        pltpu.VMEM((previous + 1,) + tiles, f32),
        pltpu.VMEM(tiles, f32),
        pltpu.VMEM(tiles, bf16),
        pltpu.VMEM(tiles, f32),
        pltpu.VMEM(tiles, f32),
        pltpu.VMEM(tiles, f32),
        pltpu.VMEM(tiles, f32),
        pltpu.VMEM(tiles, bf16),
        pltpu.VMEM(tiles, f32),
        pltpu.VMEM((size, heads * size), bf16),
        pltpu.VMEM((previous + 1, size, heads * size), bf16),
        pltpu.VMEM((previous + 1, size, heads * size), bf16),
        pltpu.VMEM((8, size), f32),
        pltpu.VMEM((8, size), f32),
        pltpu.VMEM((n_tensor, 8, size), f32),
        pltpu.VMEM((n_tensor, 8, size), f32),
        pltpu.VMEM(tiles, state_type),
        pltpu.VMEM(tiles, state_type),
        pltpu.VMEM(tiles, state_type),
        pltpu.VMEM(tiles, state_type),
        pltpu.VMEM((n_dp, 8, size), f32),
        pltpu.VMEM((n_seq, 8, size), f32),
        pltpu.VMEM((2, previous + 1, size, size), f32),
        pltpu.VMEM((2, slots, size, size), f32),
        dma((2, slots)),
        dma((2, slots)),
        dma((n_tensor,)),
        dma((n_tensor,)),
        dma((heads,)),
        dma((heads,)),
        dma((heads,)),
        dma((heads,)),
        dma((n_tensor,)),
        dma((n_tensor,)),
        dma((n_dp,)),
        dma((n_dp,)),
        dma((n_seq,)),
        dma((n_seq,)),
        dma((2, slots)),
        dma((2, slots)),
    ]
    layer_output, query_grads, key_gradient, value_gradient, gain_grads = pl.pallas_call(
        functools.partial(kernel, (n_seq, n_dp, n_tensor, previous, heads)),
        out_shape=outputs,
        in_specs=[vmem, vmem, vmem, smem] + [vmem] * 6,
        out_specs=(vmem,) * 5,
        scratch_shapes=scratch,
        compiler_params=pltpu.CompilerParams(
            collective_id=0, has_side_effects=True, vmem_limit_bytes=40 * 1024 * 1024
        ),
        name="layer_pair",
    )(
        attention_queries,
        attention_keys,
        attention_values,
        key_window_length,
        norm_gain.reshape(heads, size),
        spike_levels.reshape(heads, size),
        lin_queries,
        lin_keys,
        decay_logs,
        cotangent,
    )
    return (layer_output, query_grads, key_gradient, value_gradient, gain_grads.reshape(-1))


def solution(mesh):
    placed = (
        P("dp", "seq", "tensor"),
        P("dp", "seq", "tensor"),
        P("dp", "seq", "tensor"),
        P("tensor"),
        P("tensor"),
        P("tensor"),
        P("dp", "seq", "tensor"),
        P("dp", "seq", "tensor"),
        P("dp", "tensor", "seq"),
        P("dp", "seq", "tensor"),
    )
    return jax.shard_map(
        local,
        mesh=mesh,
        in_specs=placed,
        out_specs=(
            P("dp", "seq", "tensor"),
            P("dp", "seq", "tensor"),
            P("dp", "seq", "tensor"),
            P("dp", "seq", "tensor"),
            P("tensor"),
        ),
        check_vma=False,
    )
```

time: 172 us -> 30.6 us (0.18); the launches traced: 169 us -> 30.1 us
  matrix products: 46.9 us -> 0 us
  blocking collectives: 45.2 us -> 0 us
  local copies, waits for them, and re-layouts: 35.5 us -> 9.15 us
  Pallas kernels: 0 us -> 19.6 us
  other arithmetic: 19.2 us -> 0 us
  starting transfers between devices: 16 us -> 0 us
  waiting for transfers between devices: 4.14 us -> 0 us
    dot_general x56 -> x0, matrix products: 46.9 us -> none  [the longest x14 15.4 us: head_logits(): jnp.einsum('sd,kd->sk', query_rows, key_row_block, preferred_element_type...]
    psum x3 -> x0, blocking collectives: 33 us -> none  [the longest x1 15.1 us: local(): gain_grads = lax.psum(gain_part, ('seq', 'dp'))]
    pallas_call x0 -> x1, Pallas kernels: none -> 19.6 us  [local(): pl.pallas_call(functools.partial(kernel, (n_seq, n_dp, n_tensor, previous...]
    dynamic_update_slice x14 -> x0, local copies, waits for them, and re-layouts: 18.1 us -> none  [local(): heads_out, maxima, sums = lax.map(forward_head, (head_queries, kv_of_head))]
    ppermute x8 -> x0, starting transfers between devices: 16 us -> none  [passed_along(): return lax.ppermute(block, axis, route)]
    add x31 -> x0, other arithmetic: 9.17 us -> none  [the longest x14 9.07 us: head_logits(): query_pos = first_query + jnp.arange(block_rows, dtype=jnp.int32)[:, None]]
    all_gather x2 -> x0, blocking collectives: 8.31 us -> none  [entering(): pieces = jax.tree.map(lambda part: lax.all_gather(part, axis), value)]
    sub x7 -> x0, local copies, waits for them, and re-layouts: 4.95 us -> none  [backward_head(): probs = jnp.exp(logits - row_max[:, None]) / row_sum[:, None]]
  transfers between devices with their start and end apart: 8 -> 0, of which waited for: 4 -> 0; matrix products, arithmetic and copies ran while one was open for 7% -> 0% of each run, Pallas kernels for 0% -> 0%
where the time goes in v1:
time: 30.6 us; the launch traced here: 30.1 us
  Pallas kernels  19.6 us (64%)
  local copies, waits for them, and re-layouts  9.15 us (30%)
  between operations  1.34 us (4%)
    pallas_call x1, Pallas kernels, local(): pl.pallas_call(functools.partial(kernel, (n_seq, n_dp, n_tensor, previous...  19.6 us
    unnamed x24, local copies, waits for them, and re-layouts  9.15 us

profile of v1, /device:TPU:1, one launch (start us, length us, event | category | flops | bytes accessed | tf_op | source)
XLA Modules:
  0.0 30.1 jit_solution(10599552582048812697)
XLA Ops:
  0.6 0.0 copy-start.8
  1.3 0.0 copy-start.7
  1.3 0.0 copy-done.8
  1.3 0.0 copy-start.6
  1.3 0.6 %copy-done.7 = s32[896]{0:T(1024)S(1)} copy-done((s32[896]{0:T(1024)S(1)}, s32[896]{0:T(1024)}, u32[]{:S(2)}) %copy-start.7) | copy-done | bytes 3608
  2.0 0.0 copy-done.6
  2.0 0.0 copy-start
  2.0 0.9 %copy-done = bf16[1,128,896]{2,1,0:T(8,128)(2,1)S(1)} copy-done((bf16[1,128,896]{2,1,0:T(8,128)(2,1)S(1)}, bf16[1,128,896]{2,1,0:T(8,128)(2,1)}, u32[]{:S(2)}) %copy-start) | copy-done | bytes 229400
  2.9 0.0 copy-start.1
  3.0 0.9 %copy-done.1 = bf16[1,128,896]{2,1,0:T(8,128)(2,1)S(1)} copy-done((bf16[1,128,896]{2,1,0:T(8,128)(2,1)S(1)}, bf16[1,128,896]{2,1,0:T(8,128)(2,1)}, u32[]{:S(2)}) %copy-start.1) | copy-done | bytes 229400
  3.9 0.0 copy-start.2
  3.9 0.9 %copy-done.2 = bf16[1,128,896]{2,1,0:T(8,128)(2,1)S(1)} copy-done((bf16[1,128,896]{2,1,0:T(8,128)(2,1)S(1)}, bf16[1,128,896]{2,1,0:T(8,128)(2,1)}, u32[]{:S(2)}) %copy-start.2) | copy-done | bytes 229400
  4.8 0.0 copy-start.3
  4.8 0.9 %copy-done.3 = bf16[1,128,896]{2,1,0:T(8,128)(2,1)S(1)} copy-done((bf16[1,128,896]{2,1,0:T(8,128)(2,1)S(1)}, bf16[1,128,896]{2,1,0:T(8,128)(2,1)}, u32[]{:S(2)}) %copy-start.3) | copy-done | bytes 229400
  5.8 0.0 copy-start.4
  5.8 0.8 %copy-done.4 = bf16[1,128,128]{2,1,0:T(8,128)(2,1)S(1)} copy-done((bf16[1,128,128]{2,1,0:T(8,128)(2,1)S(1)}, bf16[1,128,128]{2,1,0:T(8,128)(2,1)}, u32[]{:S(2)}) %copy-start.4) | copy-done | bytes 32792
  6.5 0.0 copy-start.5
  6.5 0.8 %copy-done.5 = bf16[1,128,128]{2,1,0:T(8,128)(2,1)S(1)} copy-done((bf16[1,128,128]{2,1,0:T(8,128)(2,1)S(1)}, bf16[1,128,128]{2,1,0:T(8,128)(2,1)}, u32[]{:S(2)}) %copy-start.5) | copy-done | bytes 32792
  7.3 19.6 %layer_pair.1 = (bf16[1,128,896]{2,1,0:T(8,128)(2,1)S(1)}, bf16[1,128,896]{2,1,0:T(8,128)(2,1)S(1)}, bf16[1,128,128]{2,1,0:T(8,128)(2,1)S(1)}, bf16[1,128,128]{2,1,0:T(8,128)(2,1)S(1)}, f32[7,128]{1,0:T(8,128)S(1)}) custom-call(bf16[1,128,896]{2,1,0:T(8,128)(2,1)S(1)} %copy-done, bf16[1,128,128]{2,1,0:T(8,128)(2,1)S(1)} %copy-done.4, ...), custom_call_target="tpu_custom_call" | custom-call | tf_op jit(solution)/shard_map/layer_pair/pallas_call | solution.py:598
  26.9 0.7 %copy.22 = bf16[1,128,896]{2,1,0:T(8,128)(2,1)} copy(bf16[1,128,896]{2,1,0:T(8,128)(2,1)S(1)} %get-tuple-element.20) | data formatting | bytes 458752
  27.6 0.7 %copy.23 = bf16[1,128,896]{2,1,0:T(8,128)(2,1)} copy(bf16[1,128,896]{2,1,0:T(8,128)(2,1)S(1)} %get-tuple-element.21) | data formatting | bytes 458752
  28.3 0.6 %copy.24 = bf16[1,128,128]{2,1,0:T(8,128)(2,1)} copy(bf16[1,128,128]{2,1,0:T(8,128)(2,1)S(1)} %get-tuple-element.22) | data formatting | bytes 65536
  28.9 0.6 %copy.25 = bf16[1,128,128]{2,1,0:T(8,128)(2,1)} copy(bf16[1,128,128]{2,1,0:T(8,128)(2,1)S(1)} %get-tuple-element.23) | data formatting | bytes 65536
  29.5 0.6 %copy.26 = f32[896]{0:T(1024)} copy(f32[896]{0:T(1024)S(1)} %bitcast.5) | data formatting | bytes 7168
  (1 shorter events, 0.0 us)
Async XLA Ops:
  0.6 0.7 %copy-start.8 = (f32[1,7,128]{2,0,1:T(1,128)S(1)}, f32[1,7,128]{2,0,1:T(1,128)}, u32[]{:S(2)}) copy-start(f32[1,7,128]{2,0,1:T(1,128)} %param.18) | copy-start | bytes 10756
  1.3 0.7 %copy-start.7 = (s32[896]{0:T(1024)S(1)}, s32[896]{0:T(1024)}, u32[]{:S(2)}) copy-start(s32[896]{0:T(1024)} %param.15) | copy-start | bytes 10756
  1.3 0.7 %copy-start.6 = (f32[896]{0:T(1024)S(1)}, f32[896]{0:T(1024)}, u32[]{:S(2)}) copy-start(f32[896]{0:T(1024)} %param.14) | copy-start | bytes 10756
  2.0 0.9 %copy-start = (bf16[1,128,896]{2,1,0:T(8,128)(2,1)S(1)}, bf16[1,128,896]{2,1,0:T(8,128)(2,1)}, u32[]{:S(2)}) copy-start(bf16[1,128,896]{2,1,0:T(8,128)(2,1)} %q_ref.1) | copy-start | bytes 688132
  2.9 0.9 %copy-start.1 = (bf16[1,128,896]{2,1,0:T(8,128)(2,1)S(1)}, bf16[1,128,896]{2,1,0:T(8,128)(2,1)}, u32[]{:S(2)}) copy-start(bf16[1,128,896]{2,1,0:T(8,128)(2,1)} %lq_ref.1) | copy-start | bytes 688132
  3.9 0.9 %copy-start.2 = (bf16[1,128,896]{2,1,0:T(8,128)(2,1)S(1)}, bf16[1,128,896]{2,1,0:T(8,128)(2,1)}, u32[]{:S(2)}) copy-start(bf16[1,128,896]{2,1,0:T(8,128)(2,1)} %lk_ref.1) | copy-start | bytes 688132
  4.8 0.9 %copy-start.3 = (bf16[1,128,896]{2,1,0:T(8,128)(2,1)S(1)}, bf16[1,128,896]{2,1,0:T(8,128)(2,1)}, u32[]{:S(2)}) copy-start(bf16[1,128,896]{2,1,0:T(8,128)(2,1)} %ct_ref.1) | copy-start | bytes 688132
  5.8 0.8 %copy-start.4 = (bf16[1,128,128]{2,1,0:T(8,128)(2,1)S(1)}, bf16[1,128,128]{2,1,0:T(8,128)(2,1)}, u32[]{:S(2)}) copy-start(bf16[1,128,128]{2,1,0:T(8,128)(2,1)} %k_ref.1) | copy-start | bytes 98308
  6.5 0.8 %copy-start.5 = (bf16[1,128,128]{2,1,0:T(8,128)(2,1)S(1)}, bf16[1,128,128]{2,1,0:T(8,128)(2,1)}, u32[]{:S(2)}) copy-start(bf16[1,128,128]{2,1,0:T(8,128)(2,1)} %v_ref.1) | copy-start | bytes 98308

commit v2 on v1

--- a/solution.py
+++ b/solution.py
@@ -11,6 +11,7 @@
 HEAD_SIZE = 128
 D = 3584
 LONGEST_WINDOW = 512
+VMEM_LIMIT = 63 * 1024 * 1024
 
 MESH = pl.DeviceIdType.MESH
 f32 = jnp.float32
@@ -33,21 +34,37 @@
 
 def kernel(
     sizes,
+    q_hbm,
+    k_hbm,
+    v_hbm,
+    window_ref,
+    gain_hbm,
+    level_hbm,
+    lq_hbm,
+    lk_hbm,
+    decay_hbm,
+    ct_hbm,
+    out_hbm,
+    qg_hbm,
+    kg_hbm,
+    vg_hbm,
+    gg_hbm,
+    out_ref,
+    qg_ref,
+    kg_ref,
+    vg_ref,
+    gg_ref,
+    store_sems,
     q_ref,
     k_ref,
     v_ref,
-    window_ref,
     gain_ref,
     level_ref,
     lq_ref,
     lk_ref,
     decay_ref,
     ct_ref,
-    out_ref,
-    qg_ref,
-    kg_ref,
-    vg_ref,
-    gg_ref,
+    fetch_sems,
     pair_prev,
     probs,
     heads_out,
@@ -105,6 +122,36 @@
                 device_id={axis: lax.rem(me + step, count)},
                 device_id_type=MESH,
             )
+    fetches = [
+        pltpu.make_async_copy(source, target, fetch_sems.at[i])
+        for i, (source, target) in enumerate(
+            (
+                (k_hbm, k_ref),
+                (q_hbm, q_ref),
+                (v_hbm, v_ref),
+                (decay_hbm, decay_ref),
+                (gain_hbm, gain_ref),
+                (level_hbm, level_ref),
+                (lk_hbm, lk_ref),
+                (lq_hbm, lq_ref),
+                (ct_hbm, ct_ref),
+            )
+        )
+    ]
+    for fetch in fetches:
+        fetch.start()
+    stores = [
+        pltpu.make_async_copy(source, target, store_sems.at[i])
+        for i, (source, target) in enumerate(
+            (
+                (out_ref, out_hbm),
+                (qg_ref, qg_hbm),
+                (kg_ref, kg_hbm),
+                (vg_ref, vg_hbm),
+                (gg_ref, gg_hbm),
+            )
+        )
+    ]
     pl.semaphore_wait(barrier, n_seq + n_dp + n_tensor - 3)
 
     def remote(src, dst, send, recv, axis, target):
@@ -151,7 +198,7 @@
         return start, wait, drain
 
     def pair_copy(index, distance):
-        source = (k_ref, v_ref)[index].at[0]
+        source = (k_hbm, v_hbm)[index].at[0]
         return remote(
             source,
             pair_prev.at[index, distance - 1],
@@ -187,6 +234,8 @@
     column_index = lax.broadcasted_iota(jnp.int32, (size, size), 1)
     causal = row_index <= column_index
     window = window_ref[0]
+    for fetch in fetches[:3]:
+        fetch.wait()
     keys = k_ref[0]
     values = v_ref[0]
     keys_turned = turned(keys).astype(bf16)
@@ -251,7 +300,9 @@
     )
     start()
 
-    logs = decay_ref[0]
+    for fetch in fetches[3:]:
+        fetch.wait()
+    logs = decay_ref[:, 0, :]
     upper = jnp.where(causal, 1.0, 0.0)
     cumulative = jnp.dot(logs, upper, precision=precise, preferred_element_type=f32)
     whole = jnp.dot(
@@ -368,6 +419,7 @@
     for h in range(heads):
         out_ref[0, :, cols[h]] = work[h].T.astype(bf16)
         work[h] = nt(spikes_buf[h], decayed[h])
+    stores[0].start()
 
     if n_seq > 1:
 
@@ -473,11 +525,13 @@
                     query_grad = query_grad + nn(earlier[d], logit_grads[d + 1, :, cols[h]])
                 qg_ref[0, :, cols[h]] = query_grad.T.astype(bf16)
 
+    stores[1].start()
     key_sum, value_sum = pair_sums(0)
     pair_out[0, previous] = key_sum
     pair_out[1, previous] = value_sum
     wait_seq()
     gg_ref[...] = sum(gain_sum_slots[i] for i in range(n_seq))[:heads]
+    stores[4].start()
 
     for distance in range(1, previous + 1):
 
@@ -491,6 +545,8 @@
 
     kg_ref[0] = pair_out[0, previous].astype(bf16)
     vg_ref[0] = pair_out[1, previous].astype(bf16)
+    stores[2].start()
+    stores[3].start()
 
     for distance in range(1, previous + 1):
 
@@ -520,6 +576,20 @@
     drain_slopes()
     drain_dp()
     drain_seq()
+    for store in stores:
+        store.wait()
+
+
+def write_out(*refs):
+    sources, targets, sems = refs[:5], refs[5:10], refs[10]
+    copies = [
+        pltpu.make_async_copy(source, target, sems.at[i])
+        for i, (source, target) in enumerate(zip(sources, targets))
+    ]
+    for copy in copies:
+        copy.start()
+    for copy in copies:
+        copy.wait()
 
 
 def local(
@@ -541,7 +611,7 @@
     slots = max(previous, 1)
     state_type = bf16 if n_seq == 2 else f32
     size = HEAD_SIZE
-    vmem = pl.BlockSpec(memory_space=pltpu.VMEM)
+    hbm = pl.BlockSpec(memory_space=pltpu.HBM)
     smem = pl.BlockSpec(memory_space=pltpu.SMEM)
     tiles = (heads, size, size)
     dma = pltpu.SemaphoreType.DMA
@@ -552,7 +622,25 @@
         jax.ShapeDtypeStruct(attention_keys.shape, bf16),
         jax.ShapeDtypeStruct((heads, size), f32),
     )
+    wide = pltpu.VMEM(attention_queries.shape, bf16)
+    narrow = pltpu.VMEM(attention_keys.shape, bf16)
     scratch = [
+        wide,
+        wide,
+        narrow,
+        narrow,
+        pltpu.VMEM((heads, size), f32),
+        dma((5,)),
+        wide,
+        narrow,
+        narrow,
+        pltpu.VMEM((heads, size), f32),
+        pltpu.VMEM((heads, size), jnp.int32),
+        wide,
+        wide,
+        pltpu.VMEM((heads, 1, size), f32),
+        wide,
+        dma((9,)),
         pltpu.VMEM((2, slots, size, size), bf16),
         pltpu.VMEM((previous + 1,) + tiles, f32),
         pltpu.VMEM(tiles, f32),
@@ -595,14 +683,14 @@
         dma((2, slots)),
         dma((2, slots)),
     ]
-    layer_output, query_grads, key_gradient, value_gradient, gain_grads = pl.pallas_call(
+    results = pl.pallas_call(
         functools.partial(kernel, (n_seq, n_dp, n_tensor, previous, heads)),
         out_shape=outputs,
-        in_specs=[vmem, vmem, vmem, smem] + [vmem] * 6,
-        out_specs=(vmem,) * 5,
+        in_specs=[hbm, hbm, hbm, smem] + [hbm] * 6,
+        out_specs=(hbm,) * 5,
         scratch_shapes=scratch,
         compiler_params=pltpu.CompilerParams(
-            collective_id=0, has_side_effects=True, vmem_limit_bytes=40 * 1024 * 1024
+            collective_id=0, has_side_effects=True, vmem_limit_bytes=VMEM_LIMIT
         ),
         name="layer_pair",
     )(
@@ -614,9 +702,18 @@
         spike_levels.reshape(heads, size),
         lin_queries,
         lin_keys,
-        decay_logs,
+        decay_logs.reshape(heads, 1, rows),
         cotangent,
     )
+    layer_output, query_grads, key_gradient, value_gradient, gain_grads = pl.pallas_call(
+        write_out,
+        out_shape=outputs,
+        in_specs=[hbm] * 5,
+        out_specs=(hbm,) * 5,
+        scratch_shapes=[dma((5,))],
+        compiler_params=pltpu.CompilerParams(vmem_limit_bytes=VMEM_LIMIT),
+        name="write_out",
+    )(*results)
     return (layer_output, query_grads, key_gradient, value_gradient, gain_grads.reshape(-1))
 
 

time: 30.6 us -> 38.9 us (1.27); the launches traced: 30.1 us -> 38.8 us
  Pallas kernels: 19.6 us -> 37.5 us
  local copies, waits for them, and re-layouts: 9.15 us -> 0 us
    pallas_call x0 -> x1, Pallas kernels: none -> 17.1 us  [local(): pl.pallas_call(write_out, out_shape=outputs, in_specs=[hbm] * 5, out_spec...]
    unnamed x24 -> x0, local copies, waits for them, and re-layouts: 9.15 us -> none
    pallas_call x1, Pallas kernels: 19.6 us -> 20.4 us  [local(): pl.pallas_call(functools.partial(kernel, (n_seq, n_dp, n_tensor, previous...]
where the time goes in v2:
time: 38.9 us; the launch traced here: 38.8 us
  Pallas kernels  37.5 us (96%)
  between operations  1.29 us (3%)
    pallas_call x1, Pallas kernels, local(): pl.pallas_call(functools.partial(kernel, (n_seq, n_dp, n_tensor, previous...  20.4 us
    pallas_call x1, Pallas kernels, local(): pl.pallas_call(write_out, out_shape=outputs, in_specs=[hbm] * 5, out_spec...  17.1 us

profile of v2, /device:TPU:1, one launch (start us, length us, event | category | flops | bytes accessed | tf_op | source)
XLA Modules:
  0.0 38.8 jit_solution(15118617874568388496)
XLA Ops:
  1.3 20.4 %layer_pair.1 = (bf16[1,128,896]{2,1,0:T(8,128)(2,1)}, bf16[1,128,896]{2,1,0:T(8,128)(2,1)}, bf16[1,128,128]{2,1,0:T(8,128)(2,1)}, bf16[1,128,128]{2,1,0:T(8,128)(2,1)}, f32[7,128]{1,0:T(8,128)}) custom-call(bf16[1,128,896]{2,1,0:T(8,128)(2,1)} %q_hbm.1, bf16[1,128,128]{2,1,0:T(8,128)(2,1)} %k_hbm.1, bf16[1,128,128]{2,1,0:T(8,128)(2,1)} %v_hbm.1, ...), custom_call_target="tpu_custom_call" | custom-call | tf_op jit(solution)/shard_map/layer_pair/pallas_call | solution.py:686
  21.6 17.1 %write_out.1 = (bf16[1,128,896]{2,1,0:T(8,128)(2,1)}, bf16[1,128,896]{2,1,0:T(8,128)(2,1)}, bf16[1,128,128]{2,1,0:T(8,128)(2,1)}, bf16[1,128,128]{2,1,0:T(8,128)(2,1)}, f32[7,128]{1,0:T(8,128)}) custom-call(bf16[1,128,896]{2,1,0:T(8,128)(2,1)} %get-tuple-element.15.refs_0_, bf16[1,128,896]{2,1,0:T(8,128)(2,1)} %get-tuple-element.16.refs_1_, ...), custom_call_target="tpu_custom_call" | custom-call | tf_op jit(solution)/shard_map/write_out/pallas_call | solution.py:708

commit v3 on v2

--- a/solution.py
+++ b/solution.py
@@ -72,6 +72,7 @@
     ct_turned,
     gain_cols,
     level_cols,
+    ratio_cols,
     bounded_buf,
     spikes_buf,
     work,
@@ -316,6 +317,7 @@
         gain_rows = jnp.broadcast_to(gain_ref[h : h + 1, :], (size, size))
         level_cols[h] = level_rows.T
         gain_cols[h] = gain_rows.T
+        ratio_cols[h] = (gain_rows / level_rows).T
         ct_turned[h] = turned(ct_ref[0, :, cols[h]])
         along = jnp.broadcast_to(cumulative[h : h + 1, :], (size, size))
         gaps = jnp.where(causal, along - along.T, -jnp.inf)
@@ -324,121 +326,116 @@
 
     wait_squares()
     square_sum = sum(square_slots[i] for i in range(n_tensor))[:1]
-    inverse = 1.0 / jnp.sqrt(square_sum / D + epsilon)
-
-    def state_copy(h):
+    inverse = lax.rsqrt(square_sum / D + epsilon)
+
+    half = (heads + 1) // 2
+    groups = [range(half), range(half, heads)]
+
+    def state_copy(g):
+        part = pl.ds(groups[g][0], len(groups[g]))
         return remote(
-            state_out.at[h],
-            state_in.at[h],
-            state_send.at[h],
-            state_recv.at[h],
+            state_out.at[part],
+            state_in.at[part],
+            state_send.at[g],
+            state_recv.at[g],
             "seq",
             lax.rem(seq + 1, n_seq),
         )
 
-    def after_copy(h):
+    def after_copy(g):
+        part = pl.ds(groups[g][0], len(groups[g]))
         return remote(
-            after_out.at[h],
-            after_in.at[h],
-            after_send.at[h],
-            after_recv.at[h],
+            after_out.at[part],
+            after_in.at[part],
+            after_send.at[g],
+            after_recv.at[g],
             "seq",
             lax.rem(seq + n_seq - 1, n_seq),
         )
 
-    for h in range(heads):
-        normed = heads_out[h] * inverse
-        heads_out[h] = normed
-        bounded = jnp.tanh(normed * gain_cols[h] / level_cols[h])
-        bounded_buf[h] = bounded
-        spikes = (level_cols[h] * bounded).astype(bf16)
-        spikes_buf[h] = spikes
-        fading = (spikes.astype(f32) * tail[h : h + 1]).astype(bf16)
-        state_out[h] = nn(fading, lk_ref[0, :, cols[h]]).astype(state_out.dtype)
-        if n_seq == 2:
+    for g, group in enumerate(groups):
+        for h in group:
+            normed = heads_out[h] * inverse
+            heads_out[h] = normed
+            bounded = jnp.tanh(normed * ratio_cols[h])
+            bounded_buf[h] = bounded
+            spikes = (level_cols[h] * bounded).astype(bf16)
+            spikes_buf[h] = spikes
+            fading = (spikes.astype(f32) * tail[h : h + 1]).astype(bf16)
+            state_out[h] = nn(fading, lk_ref[0, :, cols[h]]).astype(state_out.dtype)
+        if n_seq > 1:
 
             @pl.when(seq == 0)
             def _():
-                state_copy(h).start()
+                state_copy(g).start()
 
     for h in range(heads):
         work[h] = nn(spikes_buf[h], decayed[h])
 
-    if n_seq > 2:
-
-        @pl.when(seq == 0)
-        def _():
-            for h in range(heads):
-                state_copy(h).start()
-
     if n_seq > 1:
 
         @pl.when(seq > 0)
         def _():
-            for h in range(heads):
-                state_copy(h).wait_recv()
+            for g, group in enumerate(groups):
+                state_copy(g).wait_recv()
                 if n_seq > 2:
-                    state_out[h] = (
-                        block_decay[h : h + 1] * state_in[h].astype(f32) + state_out[h].astype(f32)
-                    ).astype(state_out.dtype)
+                    for h in group:
+                        state_out[h] = (
+                            block_decay[h : h + 1] * state_in[h].astype(f32)
+                            + state_out[h].astype(f32)
+                        ).astype(state_out.dtype)
 
                     @pl.when(seq < n_seq - 1)
                     def _():
-                        state_copy(h).start()
-
-            for h in range(heads):
-                carried = nt(state_in[h].astype(bf16), lq_ref[0, :, cols[h]])
-                work[h] = work[h] + grown[h : h + 1] * carried
+                        state_copy(g).start()
+
+                for h in group:
+                    carried = nt(state_in[h].astype(bf16), lq_ref[0, :, cols[h]])
+                    work[h] = work[h] + grown[h : h + 1] * carried
+
+    for g, group in enumerate(groups):
+        for h in group:
+            membrane = work[h]
+            mean = jnp.sum(membrane * membrane, axis=0, keepdims=True) / size
+            scale = lax.rsqrt(mean + epsilon)
+            unit = membrane * scale
+            incoming = ct_turned[h]
+            inner = jnp.sum(incoming * unit, axis=0, keepdims=True) / size
+            grad = scale * (incoming - unit * inner)
+            ct_turned[h] = unit
+            spikes_buf[h] = grad.astype(bf16)
+            after_out[h] = nn((grad * grown[h : h + 1]).astype(bf16), lq_ref[0, :, cols[h]]).astype(
+                after_out.dtype
+            )
+        if n_seq > 1:
+
+            @pl.when(seq == n_seq - 1)
+            def _():
+                after_copy(g).start()
 
     for h in range(heads):
-        membrane = work[h]
-        mean = jnp.sum(membrane * membrane, axis=0, keepdims=True) / size
-        scale = 1.0 / jnp.sqrt(mean + epsilon)
-        unit = membrane * scale
-        incoming = ct_turned[h]
-        inner = jnp.sum(incoming * unit, axis=0, keepdims=True) / size
-        grad = scale * (incoming - unit * inner)
-        work[h] = unit
-        spikes_buf[h] = grad.astype(bf16)
-        after_out[h] = nn((grad * grown[h : h + 1]).astype(bf16), lq_ref[0, :, cols[h]]).astype(
-            after_out.dtype
-        )
-        if n_seq == 2:
-
-            @pl.when(seq == 1)
-            def _():
-                after_copy(h).start()
-
-    if n_seq > 2:
-
-        @pl.when(seq == n_seq - 1)
-        def _():
-            for h in range(heads):
-                after_copy(h).start()
-
-    for h in range(heads):
-        out_ref[0, :, cols[h]] = work[h].T.astype(bf16)
         work[h] = nt(spikes_buf[h], decayed[h])
-    stores[0].start()
 
     if n_seq > 1:
 
         @pl.when(seq < n_seq - 1)
         def _():
-            for h in range(heads):
-                after_copy(h).wait_recv()
+            for g, group in enumerate(groups):
+                after_copy(g).wait_recv()
                 if n_seq > 2:
-                    after_out[h] = (
-                        block_decay[h : h + 1] * after_in[h].astype(f32) + after_out[h].astype(f32)
-                    ).astype(after_out.dtype)
+                    for h in group:
+                        after_out[h] = (
+                            block_decay[h : h + 1] * after_in[h].astype(f32)
+                            + after_out[h].astype(f32)
+                        ).astype(after_out.dtype)
 
                     @pl.when(seq > 0)
                     def _():
-                        after_copy(h).start()
-
-            for h in range(heads):
-                later = nt(after_in[h].astype(bf16), lk_ref[0, :, cols[h]])
-                work[h] = work[h] + tail[h : h + 1] * later
+                        after_copy(g).start()
+
+                for h in group:
+                    later = nt(after_in[h].astype(bf16), lk_ref[0, :, cols[h]])
+                    work[h] = work[h] + tail[h : h + 1] * later
 
     slope_part = jnp.zeros((size, size), f32)
     for h in range(heads):
@@ -461,6 +458,10 @@
     start, wait_dp, drain_dp = exchange(gain_slots, dp_send, dp_recv, "dp", dp, n_dp)
     start()
 
+    for h in range(heads):
+        out_ref[0, :, cols[h]] = ct_turned[h].T.astype(bf16)
+    stores[0].start()
+
     wait_slopes()
     slope = sum(slope_slots[i] for i in range(n_tensor))[:1] / D
     for h in range(heads):
@@ -564,13 +565,13 @@
 
         @pl.when(seq < n_seq - 1)
         def _():
-            for h in range(heads):
-                state_copy(h).wait_send()
+            for g in range(2):
+                state_copy(g).wait_send()
 
         @pl.when(seq > 0)
         def _():
-            for h in range(heads):
-                after_copy(h).wait_send()
+            for g in range(2):
+                after_copy(g).wait_send()
 
     drain_squares()
     drain_slopes()
@@ -581,15 +582,16 @@
 
 
 def write_out(*refs):
-    sources, targets, sems = refs[:5], refs[5:10], refs[10]
-    copies = [
-        pltpu.make_async_copy(source, target, sems.at[i])
-        for i, (source, target) in enumerate(zip(sources, targets))
-    ]
-    for copy in copies:
-        copy.start()
-    for copy in copies:
-        copy.wait()
+    sources, targets, held, sems = refs[:5], refs[5:10], refs[10:15], refs[15]
+    reads = [pltpu.make_async_copy(sources[i], held[i], sems.at[0, i]) for i in range(5)]
+    writes = [pltpu.make_async_copy(held[i], targets[i], sems.at[1, i]) for i in range(5)]
+    for read in reads:
+        read.start()
+    for read, write in zip(reads, writes):
+        read.wait()
+        write.start()
+    for write in writes:
+        write.wait()
 
 
 def local(
@@ -649,6 +651,7 @@
         pltpu.VMEM(tiles, f32),
         pltpu.VMEM(tiles, f32),
         pltpu.VMEM(tiles, f32),
+        pltpu.VMEM(tiles, f32),
         pltpu.VMEM(tiles, bf16),
         pltpu.VMEM(tiles, f32),
         pltpu.VMEM((size, heads * size), bf16),
@@ -670,10 +673,10 @@
         dma((2, slots)),
         dma((n_tensor,)),
         dma((n_tensor,)),
-        dma((heads,)),
-        dma((heads,)),
-        dma((heads,)),
-        dma((heads,)),
+        dma((2,)),
+        dma((2,)),
+        dma((2,)),
+        dma((2,)),
         dma((n_tensor,)),
         dma((n_tensor,)),
         dma((n_dp,)),
@@ -710,7 +713,7 @@
         out_shape=outputs,
         in_specs=[hbm] * 5,
         out_specs=(hbm,) * 5,
-        scratch_shapes=[dma((5,))],
+        scratch_shapes=[pltpu.VMEM(out.shape, out.dtype) for out in outputs] + [dma((2, 5))],
         compiler_params=pltpu.CompilerParams(vmem_limit_bytes=VMEM_LIMIT),
         name="write_out",
     )(*results)

time: 38.9 us -> 22 us (0.57)
  Pallas kernels: 37.5 us -> 20.5 us
    pallas_call x1, Pallas kernels: 17.1 us -> 1.84 us  [local(): pl.pallas_call(write_out, out_shape=outputs, in_specs=[hbm] * 5, out_spec...]
    pallas_call x1, Pallas kernels: 20.4 us -> 18.7 us  [local(): pl.pallas_call(functools.partial(kernel, (n_seq, n_dp, n_tensor, previous...]
where the time goes in v3:
time: 22 us; the launch traced here: 21.8 us
  Pallas kernels  20.5 us (93%)
  between operations  1.29 us (6%)
    pallas_call x1, Pallas kernels, local(): pl.pallas_call(functools.partial(kernel, (n_seq, n_dp, n_tensor, previous...  18.7 us
    pallas_call x1, Pallas kernels, local(): pl.pallas_call(write_out, out_shape=outputs, in_specs=[hbm] * 5, out_spec...  1.84 us

profile of v3, /device:TPU:1, one launch (start us, length us, event | category | flops | bytes accessed | tf_op | source)
XLA Modules:
  0.0 21.8 jit_solution(9682613586609218904)
XLA Ops:
  1.3 18.7 %layer_pair.1 = (bf16[1,128,896]{2,1,0:T(8,128)(2,1)}, bf16[1,128,896]{2,1,0:T(8,128)(2,1)}, bf16[1,128,128]{2,1,0:T(8,128)(2,1)}, bf16[1,128,128]{2,1,0:T(8,128)(2,1)}, f32[7,128]{1,0:T(8,128)}) custom-call(bf16[1,128,896]{2,1,0:T(8,128)(2,1)} %q_hbm.1, bf16[1,128,128]{2,1,0:T(8,128)(2,1)} %k_hbm.1, bf16[1,128,128]{2,1,0:T(8,128)(2,1)} %v_hbm.1, ...), custom_call_target="tpu_custom_call" | custom-call | tf_op jit(solution)/shard_map/layer_pair/pallas_call | solution.py:689
  20.0 1.8 %write_out.1 = (bf16[1,128,896]{2,1,0:T(8,128)(2,1)}, bf16[1,128,896]{2,1,0:T(8,128)(2,1)}, bf16[1,128,128]{2,1,0:T(8,128)(2,1)}, bf16[1,128,128]{2,1,0:T(8,128)(2,1)}, f32[7,128]{1,0:T(8,128)}) custom-call(bf16[1,128,896]{2,1,0:T(8,128)(2,1)} %get-tuple-element.15.refs_0_, bf16[1,128,896]{2,1,0:T(8,128)(2,1)} %get-tuple-element.16.refs_1_, ...), custom_call_target="tpu_custom_call" | custom-call | tf_op jit(solution)/shard_map/write_out/pallas_call | solution.py:711

commit v4 on v3

--- a/solution.py
+++ b/solution.py
@@ -11,7 +11,8 @@
 HEAD_SIZE = 128
 D = 3584
 LONGEST_WINDOW = 512
-VMEM_LIMIT = 63 * 1024 * 1024
+VMEM_LIMIT = 62 * 1024 * 1024
+WRITE_LIMIT = 4 * 1024 * 1024
 
 MESH = pl.DeviceIdType.MESH
 f32 = jnp.float32
@@ -44,17 +45,11 @@
     lk_hbm,
     decay_hbm,
     ct_hbm,
-    out_hbm,
-    qg_hbm,
-    kg_hbm,
-    vg_hbm,
-    gg_hbm,
     out_ref,
     qg_ref,
     kg_ref,
     vg_ref,
     gg_ref,
-    store_sems,
     q_ref,
     k_ref,
     v_ref,
@@ -141,18 +136,6 @@
     ]
     for fetch in fetches:
         fetch.start()
-    stores = [
-        pltpu.make_async_copy(source, target, store_sems.at[i])
-        for i, (source, target) in enumerate(
-            (
-                (out_ref, out_hbm),
-                (qg_ref, qg_hbm),
-                (kg_ref, kg_hbm),
-                (vg_ref, vg_hbm),
-                (gg_ref, gg_hbm),
-            )
-        )
-    ]
     pl.semaphore_wait(barrier, n_seq + n_dp + n_tensor - 3)
 
     def remote(src, dst, send, recv, axis, target):
@@ -460,7 +443,6 @@
 
     for h in range(heads):
         out_ref[0, :, cols[h]] = ct_turned[h].T.astype(bf16)
-    stores[0].start()
 
     wait_slopes()
     slope = sum(slope_slots[i] for i in range(n_tensor))[:1] / D
@@ -480,10 +462,11 @@
                 logit_grad = probs[d, h] * (prob_grad - delta) * scaling
                 logit_grads[d, :, cols[h]] = logit_grad.astype(bf16)
 
-    def pair_sums(d):
-        key_sum = sum(nn(logit_grads[d, :, cols[h]], q_ref[0, :, cols[h]]) for h in range(heads))
-        value_sum = nt(weights_buf[d], out_grads[...])
-        return key_sum, value_sum
+    def key_sum(d):
+        return sum(nn(logit_grads[d, :, cols[h]], q_ref[0, :, cols[h]]) for h in range(heads))
+
+    def value_sum(d):
+        return nt(weights_buf[d], out_grads[...])
 
     @pl.when(seq == 0)
     def _():
@@ -493,16 +476,20 @@
 
         @pl.when(seq > 0)
         def _():
+            for distance in range(1, previous + 1):
+                pair_out[1, distance - 1] = value_sum(distance)
+
+                @pl.when(seq >= distance)
+                def _():
+                    grad_copy(1, distance).start()
+
             back(previous)
             for distance in range(1, previous + 1):
-                key_sum, value_sum = pair_sums(distance)
-                pair_out[0, distance - 1] = key_sum
-                pair_out[1, distance - 1] = value_sum
+                pair_out[0, distance - 1] = key_sum(distance)
 
                 @pl.when(seq >= distance)
                 def _():
                     grad_copy(0, distance).start()
-                    grad_copy(1, distance).start()
 
     wait_dp()
     gain_sum_slots[seq] = sum(gain_slots[i] for i in range(n_dp))
@@ -526,13 +513,10 @@
                     query_grad = query_grad + nn(earlier[d], logit_grads[d + 1, :, cols[h]])
                 qg_ref[0, :, cols[h]] = query_grad.T.astype(bf16)
 
-    stores[1].start()
-    key_sum, value_sum = pair_sums(0)
-    pair_out[0, previous] = key_sum
-    pair_out[1, previous] = value_sum
+    pair_out[0, previous] = key_sum(0)
+    pair_out[1, previous] = value_sum(0)
     wait_seq()
     gg_ref[...] = sum(gain_sum_slots[i] for i in range(n_seq))[:heads]
-    stores[4].start()
 
     for distance in range(1, previous + 1):
 
@@ -546,8 +530,6 @@
 
     kg_ref[0] = pair_out[0, previous].astype(bf16)
     vg_ref[0] = pair_out[1, previous].astype(bf16)
-    stores[2].start()
-    stores[3].start()
 
     for distance in range(1, previous + 1):
 
@@ -577,18 +559,12 @@
     drain_slopes()
     drain_dp()
     drain_seq()
-    for store in stores:
-        store.wait()
 
 
 def write_out(*refs):
-    sources, targets, held, sems = refs[:5], refs[5:10], refs[10:15], refs[15]
-    reads = [pltpu.make_async_copy(sources[i], held[i], sems.at[0, i]) for i in range(5)]
-    writes = [pltpu.make_async_copy(held[i], targets[i], sems.at[1, i]) for i in range(5)]
-    for read in reads:
-        read.start()
-    for read, write in zip(reads, writes):
-        read.wait()
+    sources, targets, sems = refs[:5], refs[5:10], refs[10]
+    writes = [pltpu.make_async_copy(sources[i], targets[i], sems.at[i]) for i in range(5)]
+    for write in writes:
         write.start()
     for write in writes:
         write.wait()
@@ -614,6 +590,7 @@
     state_type = bf16 if n_seq == 2 else f32
     size = HEAD_SIZE
     hbm = pl.BlockSpec(memory_space=pltpu.HBM)
+    vmem = pl.BlockSpec(memory_space=pltpu.VMEM)
     smem = pl.BlockSpec(memory_space=pltpu.SMEM)
     tiles = (heads, size, size)
     dma = pltpu.SemaphoreType.DMA
@@ -627,12 +604,6 @@
     wide = pltpu.VMEM(attention_queries.shape, bf16)
     narrow = pltpu.VMEM(attention_keys.shape, bf16)
     scratch = [
-        wide,
-        wide,
-        narrow,
-        narrow,
-        pltpu.VMEM((heads, size), f32),
-        dma((5,)),
         wide,
         narrow,
         narrow,
@@ -688,9 +659,9 @@
     ]
     results = pl.pallas_call(
         functools.partial(kernel, (n_seq, n_dp, n_tensor, previous, heads)),
-        out_shape=outputs,
+        out_shape=tuple(pltpu.VMEM(out.shape, out.dtype) for out in outputs),
         in_specs=[hbm, hbm, hbm, smem] + [hbm] * 6,
-        out_specs=(hbm,) * 5,
+        out_specs=(vmem,) * 5,
         scratch_shapes=scratch,
         compiler_params=pltpu.CompilerParams(
             collective_id=0, has_side_effects=True, vmem_limit_bytes=VMEM_LIMIT
@@ -711,10 +682,10 @@
     layer_output, query_grads, key_gradient, value_gradient, gain_grads = pl.pallas_call(
         write_out,
         out_shape=outputs,
-        in_specs=[hbm] * 5,
+        in_specs=[vmem] * 5,
         out_specs=(hbm,) * 5,
-        scratch_shapes=[pltpu.VMEM(out.shape, out.dtype) for out in outputs] + [dma((2, 5))],
-        compiler_params=pltpu.CompilerParams(vmem_limit_bytes=VMEM_LIMIT),
+        scratch_shapes=[dma((5,))],
+        compiler_params=pltpu.CompilerParams(vmem_limit_bytes=WRITE_LIMIT),
         name="write_out",
     )(*results)
     return (layer_output, query_grads, key_gradient, value_gradient, gain_grads.reshape(-1))

time: 22 us -> 20.4 us (0.927)
  Pallas kernels: 20.5 us -> 18.9 us
    pallas_call x1, Pallas kernels: 1.84 us -> 0.83 us  [local(): pl.pallas_call(write_out, out_shape=outputs, in_specs=[vmem] * 5, out_spe...]
    pallas_call x1, Pallas kernels: 18.7 us -> 18.1 us  [local(): pl.pallas_call(functools.partial(kernel, (n_seq, n_dp, n_tensor, previous...]
where the time goes in v4:
time: 20.4 us; the launch traced here: 20.2 us
  Pallas kernels  18.9 us (93%)
  between operations  1.29 us (6%)
    pallas_call x1, Pallas kernels, local(): pl.pallas_call(functools.partial(kernel, (n_seq, n_dp, n_tensor, previous...  18.1 us
    pallas_call x1, Pallas kernels, local(): pl.pallas_call(write_out, out_shape=outputs, in_specs=[vmem] * 5, out_spe...  0.83 us

profile of v4, /device:TPU:1, one launch (start us, length us, event | category | flops | bytes accessed | tf_op | source)
XLA Modules:
  0.0 20.2 jit_solution(16538031019325421672)
XLA Ops:
  1.3 18.1 %layer_pair.1 = (bf16[1,128,896]{2,1,0:T(8,128)(2,1)S(1)}, bf16[1,128,896]{2,1,0:T(8,128)(2,1)S(1)}, bf16[1,128,128]{2,1,0:T(8,128)(2,1)S(1)}, bf16[1,128,128]{2,1,0:T(8,128)(2,1)S(1)}, f32[7,128]{1,0:T(8,128)S(1)}) custom-call(bf16[1,128,896]{2,1,0:T(8,128)(2,1)} %q_hbm.1, bf16[1,128,128]{2,1,0:T(8,128)(2,1)} %k_hbm.1, bf16[1,128,128]{2,1,0:T(8,128)(2,1)} %v_hbm.1, ...), custom_call_target="tpu_custom_call" | custom-call | tf_op jit(solution)/shard_map/layer_pair/pallas_call | solution.py:660
  19.4 0.8 %write_out.1 = (bf16[1,128,896]{2,1,0:T(8,128)(2,1)}, bf16[1,128,896]{2,1,0:T(8,128)(2,1)}, bf16[1,128,128]{2,1,0:T(8,128)(2,1)}, bf16[1,128,128]{2,1,0:T(8,128)(2,1)}, f32[7,128]{1,0:T(8,128)}) custom-call(bf16[1,128,896]{2,1,0:T(8,128)(2,1)S(1)} %get-tuple-element.15.refs_0_, bf16[1,128,896]{2,1,0:T(8,128)(2,1)S(1)} %get-tuple-element.16.refs_1_, ...), custom_call_target="tpu_custom_call" | custom-call | tf_op jit(solution)/shard_map/write_out/pallas_call | solution.py:682

commit v5 on v4

--- a/solution.py
+++ b/solution.py
@@ -62,6 +62,7 @@
     fetch_sems,
     pair_prev,
     probs,
+    prob_grad_buf,
     heads_out,
     decayed,
     ct_turned,
@@ -238,22 +239,25 @@
             seen = (d + 1) * size + column_index - row_index < window
             masks.append(seen & (seq > d) if n_seq > 2 else seen)
         for h in range(heads):
-            scores = [probs[0, h]]
             for d in range(blocks):
                 score = nt(block_keys[d], q_ref[0, :, cols[h]]) * scaling
-                scores.append(jnp.where(masks[d], score, -jnp.inf))
+                probs[d + 1, h] = jnp.where(masks[d], score, -jnp.inf)
+        for h in range(heads):
+            scores = [probs[d, h] for d in range(blocks + 1)]
             top = functools.reduce(
                 jnp.maximum, [jnp.max(score, axis=0, keepdims=True) for score in scores]
             )
             exponents = [jnp.exp(score - top) for score in scores]
             total = sum(jnp.sum(exponent, axis=0, keepdims=True) for exponent in exponents)
             share = 1.0 / total
-            result = None
             for d, exponent in enumerate(exponents):
                 prob = exponent * share
                 probs[d, h] = prob
-                weights = prob.astype(bf16)
-                weights_buf[d, :, cols[h]] = weights
+                weights_buf[d, :, cols[h]] = prob.astype(bf16)
+        for h in range(heads):
+            result = None
+            for d in range(blocks + 1):
+                weights = weights_buf[d, :, cols[h]]
                 part = nn(values_turned if d == 0 else block_values[d - 1], weights)
                 result = part if result is None else result + part
             result = result.astype(bf16).astype(f32)
@@ -300,7 +304,7 @@
         gain_rows = jnp.broadcast_to(gain_ref[h : h + 1, :], (size, size))
         level_cols[h] = level_rows.T
         gain_cols[h] = gain_rows.T
-        ratio_cols[h] = (gain_rows / level_rows).T
+        ratio_cols[h] = gain_cols[h] / level_cols[h]
         ct_turned[h] = turned(ct_ref[0, :, cols[h]])
         along = jnp.broadcast_to(cumulative[h : h + 1, :], (size, size))
         gaps = jnp.where(causal, along - along.T, -jnp.inf)
@@ -453,7 +457,10 @@
     def back(blocks):
         block_values = [values] + [pair_prev[1, d] for d in range(blocks)]
         for h in range(heads):
-            prob_grads = [nn(block, out_grads[:, cols[h]]) for block in block_values]
+            for d, block in enumerate(block_values):
+                prob_grad_buf[d, h] = nn(block, out_grads[:, cols[h]])
+        for h in range(heads):
+            prob_grads = [prob_grad_buf[d, h] for d in range(blocks + 1)]
             delta = sum(
                 jnp.sum(probs[d, h] * prob_grad, axis=0, keepdims=True)
                 for d, prob_grad in enumerate(prob_grads)
@@ -615,6 +622,7 @@
         wide,
         dma((9,)),
         pltpu.VMEM((2, slots, size, size), bf16),
+        pltpu.VMEM((previous + 1,) + tiles, f32),
         pltpu.VMEM((previous + 1,) + tiles, f32),
         pltpu.VMEM(tiles, f32),
         pltpu.VMEM(tiles, bf16),

time: 20.4 us -> 20.4 us (level)
  no operation moved by 1% of the time
where the time goes in v5:
time: 20.4 us; the launch traced here: 20.2 us
  Pallas kernels  18.9 us (93%)
  between operations  1.29 us (6%)
    pallas_call x1, Pallas kernels, local(): pl.pallas_call(functools.partial(kernel, (n_seq, n_dp, n_tensor, previous...  18.1 us
    pallas_call x1, Pallas kernels, local(): pl.pallas_call(write_out, out_shape=outputs, in_specs=[vmem] * 5, out_spe...  0.83 us

profile of v5, /device:TPU:1, one launch (start us, length us, event | category | flops | bytes accessed | tf_op | source)
XLA Modules:
  0.0 20.2 jit_solution(13285783870153234292)
XLA Ops:
  1.3 18.1 %layer_pair.1 = (bf16[1,128,896]{2,1,0:T(8,128)(2,1)S(1)}, bf16[1,128,896]{2,1,0:T(8,128)(2,1)S(1)}, bf16[1,128,128]{2,1,0:T(8,128)(2,1)S(1)}, bf16[1,128,128]{2,1,0:T(8,128)(2,1)S(1)}, f32[7,128]{1,0:T(8,128)S(1)}) custom-call(bf16[1,128,896]{2,1,0:T(8,128)(2,1)} %q_hbm.1, bf16[1,128,128]{2,1,0:T(8,128)(2,1)} %k_hbm.1, bf16[1,128,128]{2,1,0:T(8,128)(2,1)} %v_hbm.1, ...), custom_call_target="tpu_custom_call" | custom-call | tf_op jit(solution)/shard_map/layer_pair/pallas_call | solution.py:668
  19.4 0.8 %write_out.1 = (bf16[1,128,896]{2,1,0:T(8,128)(2,1)}, bf16[1,128,896]{2,1,0:T(8,128)(2,1)}, bf16[1,128,128]{2,1,0:T(8,128)(2,1)}, bf16[1,128,128]{2,1,0:T(8,128)(2,1)}, f32[7,128]{1,0:T(8,128)}) custom-call(bf16[1,128,896]{2,1,0:T(8,128)(2,1)S(1)} %get-tuple-element.15.refs_0_, bf16[1,128,896]{2,1,0:T(8,128)(2,1)S(1)} %get-tuple-element.16.refs_1_, ...), custom_call_target="tpu_custom_call" | custom-call | tf_op jit(solution)/shard_map/write_out/pallas_call | solution.py:690
